TPU v7x, 32 devices: a whole 2x2x4 slice. The times are simulated.
32 devices in a mesh: shard: 8 (over z, x), tensor: 4 (over y, core).
Axes of the slice: x: 2, y: 2, z: 4, core: 2. Of those that a mesh axis runs over, the one named last changes fastest.
Arguments:
- gradient: bfloat16 [768, 3072], P('shard', 'tensor'), may hold values from -0.47851562 to 0.47851562
- moment: float32 [768, 3072], P('shard', 'tensor'), may hold values from -0.48 to 0.48
- second_moment: float32 [768, 3072], P('shard', 'tensor'), may hold values from 0.0001 to 0.01
- stat_left: float32 [768, 768], P('shard', 'tensor'), as said below
- stat_right: float32 [3072, 3072], P('shard', 'tensor'), as said below
- basis_left: float32 [768, 768], P('shard', 'tensor'), as said below
- basis_right: float32 [3072, 3072], P('shard', 'tensor'), as said below
Outputs:
- update: float32 [768, 3072], P('shard', 'tensor')
- moment_new: float32 [768, 3072], P('shard', 'tensor')
- second_new: float32 [768, 3072], P('shard', 'tensor')
- stat_left_new: float32 [768, 768], P('shard', 'tensor')
- stat_right_new: float32 [3072, 3072], P('shard', 'tensor')
- basis_left_new: float32 [768, 768], P('shard', 'tensor')
- basis_right_new: float32 [3072, 3072], P('shard', 'tensor')
Inputs may be any that keep to these rules, and one draw needn't show every extreme that they name: `stat_left`: a symmetric matrix. `stat_right`: a symmetric matrix. `basis_left`: a square matrix of full rank. `basis_right`: a square matrix of full rank.
All inputs are finite; a program needn't handle non-finite values.
Results may differ from a plain program's by a relative error of at most 0.0018.
The roundings to bfloat16 on the way count: a program that leaves them out, or rounds other values in their place, can miss the bound.
Values may be sent and summed in bfloat16 or wider, within the bound.
A program may use at most 64 MiB of HBM per device.

v0:
```python
import functools

import jax
import jax.numpy as jnp
from jax import lax
from jax.experimental import pallas as pl
from jax.experimental.pallas import tpu as pltpu
from jax.sharding import PartitionSpec as P

NS_ITERS = 2
BF16 = jnp.bfloat16
F32 = jnp.float32


def dot(a, b, ca, cb):
    return lax.dot_general(a, b, (((ca,), (cb,)), ((), ())), preferred_element_type=F32)


def pick(array, index, axis):
    return lax.dynamic_index_in_dim(array, index, axis, keepdims=False)


def part(array, index, size, axis):
    return lax.dynamic_slice_in_dim(array, index * size, size, axis)


def later_rows(rows, n_chain):
    return rows // (2 * (n_chain - 1)) // 16 * 16


def gather_kernel(n_chain, n_tensor, n_across, n_along, n_swap, pieces, *refs):
    count = n_across + n_along + n_swap
    ins, outs = refs[:count], refs[count : 2 * count]
    local_sem = refs[2 * count]
    sems = refs[2 * count + 1 :]
    s, t = lax.axis_index("shard"), lax.axis_index("tensor")
    a, b = s // 2, s % 2
    pair = (a * 2 + 1 - b, t)
    right = (lax.rem(a + 1, n_chain) * 2 + b, t)
    left = (lax.rem(a + n_chain - 1, n_chain) * 2 + b, t)
    near_t = t + 1 - 2 * (t % 2)
    far_t = lax.rem(t + n_tensor // 2, n_tensor)
    near, far = (s, near_t), (s, far_t)
    others = ([pair, right, left] if n_across else []) + ([near] if n_along else [])
    others += [far] if n_along or n_swap else []
    barrier = pltpu.get_barrier_semaphore()
    for other in others:
        pl.semaphore_signal(barrier, inc=1, device_id=other, device_id_type=pl.DeviceIdType.MESH)
    pl.semaphore_wait(barrier, len(others))

    def remote(src, dst, send_sem, recv_sem, target):
        return pltpu.make_async_remote_copy(
            src_ref=src,
            dst_ref=dst,
            send_sem=send_sem,
            recv_sem=recv_sem,
            device_id=target,
            device_id_type=pl.DeviceIdType.MESH,
        )

    def across(p, block, send, target, own=False):
        i, first, rows, _ = pieces[p]
        dst = outs[i].at[block, pl.ds(first, rows)]
        src = ins[i].at[pl.ds(first, rows)] if own else dst
        return remote(src, dst, sems[2 * p].at[send], sems[2 * p + 1].at[block], target)

    def along(i, block, send, target, own=False):
        pos = 2 * (len(pieces) + i - n_across)
        dst = outs[i].at[block]
        src = ins[i] if own else dst
        return remote(src, dst, sems[pos].at[send], sems[pos + 1].at[block], target)

    def swap(i):
        pos = 2 * (len(pieces) + i - n_across)
        return remote(ins[i], outs[i], sems[pos].at[0], sems[pos + 1].at[0], far)

    has_right, has_left = a + 1 < n_chain, a >= 1
    extra = 2 * n_chain
    order = sorted(range(len(pieces)), key=lambda p: not pieces[p][3])
    for p in order:
        pl.when(has_right)(lambda p=p: across(p, s, a, right, True).start())
        pl.when(has_left)(lambda p=p: across(p, s, extra, left, True).start())
        across(p, s, extra + 2 if pieces[p][3] else n_chain + a, pair, True).start()
    for i in range(n_across, n_across + n_along):
        along(i, t, 0, far, True).start()
        along(i, t, 1, near, True).start()
    for i in range(n_across + n_along, count):
        swap(i).start()
    locals_ = []
    for i in range(n_across + n_along):
        own = pltpu.make_async_copy(ins[i], outs[i].at[s if i < n_across else t], local_sem.at[i])
        own.start()
        locals_.append(own)
    for p in order:
        if pieces[p][3]:
            block = a * 2 + 1 - b
            across(p, block, extra + 2, pair).wait_recv()
            pl.when(has_right)(lambda p=p, block=block: across(p, block, n_chain + a, right).start())
            pl.when(has_left)(lambda p=p, block=block: across(p, block, extra + 1, left).start())

    def step(k, carry):
        for p in order:
            pair_first = pieces[p][3]
            for side in range(2 if pair_first else 1):
                col = 1 - b if side else b

                @pl.when(a - k >= 0)
                def _():
                    block = (a - k) * 2 + col
                    send = side * n_chain + a - k
                    across(p, block, send, right).wait_recv()
                    pl.when(has_right)(lambda: across(p, block, send, right).start())
                    if not pair_first:
                        across(p, block, n_chain + a - k, pair).start()

                @pl.when(a + k < n_chain)
                def _():
                    block = (a + k) * 2 + col
                    send = side * n_chain + a + k
                    across(p, block, send, left).wait_recv()
                    pl.when(has_left)(lambda: across(p, block, send, left).start())
                    if not pair_first:
                        across(p, block, n_chain + a + k, pair).start()

        return carry

    if n_across:
        lax.fori_loop(1, n_chain - 1, step, 0)
    for i in range(n_across, n_across + n_along):
        along(i, far_t, 2, near).wait_recv()
        along(i, far_t, 2, near).start()
    if n_across:
        step(n_chain - 1, 0)

        def finish(j, carry):
            for p in order:
                pair_first = pieces[p][3]
                if not pair_first:
                    across(p, j * 2 + 1 - b, n_chain + j, pair).wait_recv()
                    across(p, j * 2 + b, n_chain + j, pair).wait_send()
                for side in range(2 if pair_first else 1):
                    block = j * 2 + (1 - b if side else b)
                    send = side * n_chain + j
                    pl.when((j <= a) & has_right)(lambda: across(p, block, send, right).wait_send())
                    pl.when((j > a) & has_left)(lambda: across(p, block, send, left).wait_send())
            return carry

        lax.fori_loop(0, n_chain, finish, 0)
        for p in order:
            pl.when(has_left)(lambda p=p: across(p, s, extra, left).wait_send())
            if pieces[p][3]:
                pl.when(has_left)(lambda p=p: across(p, s, extra + 1, left).wait_send())
                across(p, s, extra + 2, pair).wait_send()
    near_far = near_t + far_t - t
    for i in range(n_across, n_across + n_along):
        along(i, near_t, 1, near).wait_recv()
        along(i, near_far, 2, near).wait_recv()
        for send in range(3):
            along(i, t, send, near).wait_send()
    for i in range(n_across + n_along, count):
        swap(i).wait()
    for own in locals_:
        own.wait()


def gather(name, across, along, swaps=(), *, n_shard, n_tensor):
    arrays = list(across) + list(along) + list(swaps)
    pieces = []
    for i, x in enumerate(across):
        later = later_rows(x.shape[0], n_shard // 2)
        pieces.append((i, 0, x.shape[0] - later, False))
        if later:
            pieces.append((i, x.shape[0] - later, later, True))
    shapes = [(n_shard, *x.shape) for x in across]
    shapes += [(n_tensor, *x.shape) for x in along] + [x.shape for x in swaps]
    counts = [(n_shard + 3, n_shard)] * len(pieces) + [(3, n_tensor)] * len(along) + [(1, 1)] * len(swaps)
    scratch = [pltpu.SemaphoreType.DMA((len(arrays),))]
    for sends, receives in counts:
        scratch += [pltpu.SemaphoreType.DMA((sends,)), pltpu.SemaphoreType.DMA((receives,))]
    return pl.pallas_call(
        functools.partial(
            gather_kernel, n_shard // 2, n_tensor, len(across), len(along), len(swaps), tuple(pieces)
        ),
        out_shape=[jax.ShapeDtypeStruct(shape, x.dtype) for shape, x in zip(shapes, arrays)],
        in_specs=[pl.BlockSpec(memory_space=pl.ANY)] * len(arrays),
        out_specs=[pl.BlockSpec(memory_space=pl.ANY)] * len(arrays),
        scratch_shapes=scratch,
        compiler_params=pltpu.CompilerParams(collective_id=name, has_side_effects=True),
        name="gather",
    )(*arrays)


def side_by_side(blocks):
    n, rows, cols = blocks.shape
    return blocks.transpose(1, 0, 2).reshape(rows, n * cols)


def stacked(blocks):
    return blocks.reshape(-1, blocks.shape[-1])


def lanes(array):
    return array.reshape(-1, 128)


def swap(array, bit, n_tensor):
    return lax.ppermute(array, "tensor", [(i, i ^ bit) for i in range(n_tensor)])


def gram_half(parts, core, n_tensor):
    half = parts.shape[1] // 2
    mine = part(parts, core, half, 1)
    other = part(parts, 1 - core, half, 1)
    return mine + swap(other.astype(BF16), 1, n_tensor).astype(F32)


def apply_gram(halves, panel, core):
    mine, other = halves
    half = mine.shape[1]
    return dot(mine, part(panel, core, half, 0), 1, 0) + dot(
        other, part(panel, 1 - core, half, 0), 1, 0
    )


def scatter_sum(terms, t, n_tensor):
    rows = terms.shape[0]
    width = terms.shape[1] // n_tensor
    terms = terms.reshape(rows, n_tensor // 2, 2, width)
    core = t % 2
    mine = pick(terms, core, 2) + swap(pick(terms, 1 - core, 2), 1, n_tensor)
    pair = t // 2
    count = n_tensor // 2
    while count > 1:
        count //= 2
        mine = mine.reshape(rows, 2, count, width)
        bit = (pair // count) % 2
        mine = pick(mine, bit, 1) + swap(pick(mine, 1 - bit, 1), 2 * count, n_tensor)
    return mine.reshape(rows, width)


def whole_sum(value, n_tensor):
    bit = 1
    while bit < n_tensor:
        value = value + swap(value, bit, n_tensor)
        bit *= 2
    return value


def make(n_shard, n_tensor):
    def per_device(gradient, moment, second_moment, stat_left, stat_right, basis_left, basis_right):
        s = lax.axis_index("shard")
        t = lax.axis_index("tensor")
        core = t % 2
        rows_left, block_hidden = gradient.shape
        rows_right = stat_right.shape[0]
        block_left = stat_left.shape[1]
        run = functools.partial(gather, n_shard=n_shard, n_tensor=n_tensor)

        moment_new = 0.9 * moment + 0.1 * gradient.astype(F32)
        third = rows_right // 3
        thirds = [part(basis_right, k, third, 0).astype(BF16) for k in range(3)]
        panel, left_blocks, right_0, grad_rows, moment_rows = run(
            0,
            [gradient, lanes(basis_left.astype(BF16)), thirds[0]],
            [gradient, moment_new.astype(BF16)],
        )
        panel = stacked(panel)
        first = s * rows_right
        owner = first // block_hidden
        strip = lax.dynamic_slice_in_dim(panel, first - owner * block_hidden, rows_right, 1)
        right_1, strips, left = run(1, [thirds[1]], [strip, lanes(left_blocks.reshape(-1, block_left))])
        left = side_by_side(left.reshape(n_tensor, n_shard * rows_left, block_left))
        strip = pick(strips, owner, 0)
        stat_right_new = 0.95 * stat_right + 0.05 * dot(strip, panel, 0, 0)
        cross_left = scatter_sum(dot(gradient, panel, 1, 1), t, n_tensor)
        stat_left_new = 0.95 * stat_left + 0.05 * cross_left
        right_2, stat_left_columns, stat_right_rows = run(
            2, [thirds[2], lanes(stat_left_new.astype(BF16))], [stat_right_new.astype(BF16)]
        )
        right_columns = stacked(jnp.concatenate([right_0, right_1, right_2], axis=1))

        power = dot(side_by_side(stat_right_rows), right_columns, 1, 0)
        power_half = power.astype(BF16)
        square = jnp.full((8, 128), jnp.sum(power * power), F32)
        grad_right = dot(side_by_side(grad_rows), right_columns, 1, 0).astype(BF16)
        moment_right = dot(side_by_side(moment_rows), right_columns, 1, 0).astype(BF16)
        power_panel, squares = run(3, [power_half, square], [])
        power_panel = stacked(power_panel)

        square = whole_sum(jnp.sum(squares[:, 0, 0]), n_tensor)
        scale = 1.0 / jnp.sqrt(square + 1e-06)
        mine = gram_half(dot(power_half, power_panel, 1, 1), core, n_tensor)
        grad_right, moment_right, stat_left_all, there = run(
            4, [grad_right, moment_right], [lanes(stat_left_columns.reshape(-1, 128))], [mine.astype(BF16)]
        )
        mine = (((mine + there.astype(F32)) * scale) * scale).astype(BF16)
        halves = mine, swap(mine, 1, n_tensor)
        iterate = scale * (1.5 * power - 0.5 * apply_gram(halves, power_panel, core))

        basis_strip = part(left, s, rows_left, 1)
        grad_turned = dot(basis_strip, stacked(grad_right), 0, 0)
        moment_turned = dot(basis_strip, stacked(moment_right), 0, 0)
        second_new = 0.95 * second_moment + 0.05 * grad_turned * grad_turned
        scaled = (moment_turned / (jnp.sqrt(second_new) + 1e-08)).astype(BF16)
        back_half = scatter_sum(dot(scaled, right_columns, 1, 1), t, n_tensor).astype(BF16)

        def left_basis():
            stat_all = side_by_side(stat_left_all.reshape(n_tensor, n_shard * rows_left, block_left))
            power_left = dot(stat_all, left, 1, 0)
            iterate_left = power_left / jnp.sqrt(jnp.sum(power_left * power_left) + 1e-06)
            for step in range(NS_ITERS):
                left_half = iterate_left.astype(BF16)
                if step < NS_ITERS - 1:
                    gram = dot(left_half, left_half, 1, 1).astype(BF16)
                    iterate_left = 1.5 * iterate_left - 0.5 * dot(gram, left_half, 1, 0)
                else:
                    gram = dot(part(left_half, s, rows_left, 0), left_half, 1, 1).astype(BF16)
                    own = part(part(iterate_left, s, rows_left, 0), t, block_left, 1)
                    iterate_left = 1.5 * own - 0.5 * dot(gram, part(left_half, t, block_left, 1), 1, 0)
            return iterate_left

        update = None
        for step in range(NS_ITERS - 1):
            iterate_half = iterate.astype(BF16)
            sent = [iterate_half] + ([back_half] if step == 0 else [])
            gathered = run(5 + step, sent, [])
            iterate_panel = stacked(gathered[0])
            if step == 0:
                update = dot(part(left, s, rows_left, 0), stacked(gathered[1]), 1, 0)
            mine = gram_half(dot(iterate_half, iterate_panel, 1, 1), core, n_tensor)
            there = swap(mine.astype(BF16), n_tensor // 2, n_tensor)
            if step == NS_ITERS - 2:
                there, iterate_left, update = lax.optimization_barrier((there, left_basis(), update))
            mine = (mine + there.astype(F32)).astype(BF16)
            halves = mine, swap(mine, 1, n_tensor)
            iterate = 1.5 * iterate - 0.5 * apply_gram(halves, iterate_panel, core)

        return (
            update,
            moment_new,
            second_new,
            stat_left_new,
            stat_right_new,
            iterate_left,
            iterate,
        )

    return per_device


def solution(mesh):
    spec = P("shard", "tensor")
    return jax.shard_map(
        make(mesh.shape["shard"], mesh.shape["tensor"]),
        mesh=mesh,
        in_specs=(spec,) * 7,
        out_specs=(spec,) * 7,
        check_vma=False,
    )
```

profile of v0, /device:TPU:0, one launch (start us, length us, event | category | flops | bytes accessed | tf_op | source)
XLA Modules:
  0.0 419.2 jit_solution(13756254242423923847)
XLA Ops:
  0.7 0.9 convert_element_type.80
  1.6 0.7 reshape.86.refs_1_
  2.3 1.4 convert.5
  3.7 0.8 fusion.63
  4.5 0.8 fusion.62
  5.3 41.9 %gather.6 = (bf16[8,96,768]{2,1,0:T(8,128)(2,1)}, bf16[8,144,128]{2,1,0:T(8,128)(2,1)}, bf16[8,128,768]{2,1,0:T(8,128)(2,1)}, bf16[4,96,768]{2,1,0:T(8,128)(2,1)}, bf16[4,96,768]{2,1,0:T(8,128)(2,1)}) custom-call(bf16[96,768]{1,0:T(8,128)(2,1)} %refs_3_.1, bf16[144,128]{1,0:T(8,128)(2,1)} %reshape.86.refs_1_, bf16[128,768]{1,0:T(8,128)(2,1)} %get-tuple-element.59.refs_2_, ...), custom_call_target="tpu_custom_call" | custom-call | tf_op jit(solution)/shard_map/gather/pallas_call | solution.py:180
  47.3 1.8 convolution_bitcast_fusion
  49.1 0.4 reshape.88
  49.5 0.3 constant_dynamic-slice_fusion.4
  50.0 0.3 copy-done.2
  50.3 0.9 constant_dynamic-slice_fusion.1.refs_1_
  51.2 35.9 %gather.7 = (bf16[8,128,768]{2,1,0:T(8,128)(2,1)}, bf16[4,768,384]{2,1,0:T(8,128)(2,1)}, bf16[4,1152,128]{2,1,0:T(8,128)(2,1)}) custom-call(bf16[128,768]{1,0:T(8,128)(2,1)} %get-tuple-element.58.refs_0_, bf16[768,384]{1,0:T(8,128)(2,1)} %constant_dynamic-slice_fusion.1.refs_1_, bf16[1152,128]{1,0:T(8,128)(2,1)} %bitcast.98), custom_call_target="tpu_custom_call" | custom-call | tf_op jit(solution)/shard_map/gather/pallas_call | solution.py:180
  87.1 3.1 fusion.64
  90.2 1.4 constant_dynamic-update-slice_fusion.2
  91.6 1.2 collective-permute-start.1
  92.8 1.3 constant_dynamic-update-slice_fusion.1
  94.1 2.2 collective-permute-done.1
  96.3 0.7 fusion.61
  97.0 0.7 reshape.89.refs_1_
  97.7 29.1 %gather.8 = (bf16[8,128,768]{2,1,0:T(8,128)(2,1)}, bf16[8,144,128]{2,1,0:T(8,128)(2,1)}, bf16[4,384,768]{2,1,0:T(8,128)(2,1)}) custom-call(bf16[128,768]{1,0:T(8,128)(2,1)} %get-tuple-element.57.refs_0_, bf16[144,128]{1,0:T(8,128)(2,1)} %reshape.89.refs_1_, bf16[384,768]{1,0:T(8,128)(2,1)} %get-tuple-element.62.refs_2_), custom_call_target="tpu_custom_call" | custom-call | tf_op jit(solution)/shard_map/gather/pallas_call | solution.py:180
  126.8 3.0 copy.18
  129.8 2.7 constant_dynamic-update-slice_fusion
  132.5 5.8 %multiply_reduce_fusion.1 = (f32[]{:T(128)}, bf16[384,768]{1,0:T(8,128)(2,1)}, f32[384,768]{1,0:T(8,128)S(1)}) fusion(bf16[384,3072]{0,1:T(8,128)(2,1)S(1)} %bitcast.73, bf16[3072,768]{1,0:T(8,128)(2,1)} %bitcast.9), kind=kOutput, calls=%fused_computation.26 | convolution fusion | flops 1812824064 | bytes 8847364 | tf_op jit(solution)/shard_map/dot_general | solution.py:16
  138.3 1.2 broadcast_in_dim.3.refs_1_
  139.6 55.9 %gather.9 = (bf16[8,384,768]{2,1,0:T(8,128)(2,1)}, f32[8,8,128]{2,1,0:T(8,128)}) custom-call(bf16[384,768]{1,0:T(8,128)(2,1)} %get-tuple-element.56.refs_0_, f32[8,128]{1,0:T(8,128)} %broadcast_in_dim.3.refs_1_), custom_call_target="tpu_custom_call" | custom-call | tf_op jit(solution)/shard_map/gather/pallas_call | solution.py:180
  195.5 4.5 %fusion.69 = f32[384,3072]{1,0:T(8,128)S(1)} fusion(bf16[384,768]{1,0:T(8,128)(2,1)} %get-tuple-element.56.refs_0_, bf16[3072,768]{1,0:T(8,128)(2,1)} %bitcast.88), kind=kOutput, calls=%fused_computation.86 | convolution fusion | flops 1811939328 | bytes 10027008 | tf_op jit(solution)/shard_map/dot_general | solution.py:16
  200.0 2.1 copy-done
  202.2 1.2 dynamic-slice_convert_fusion.1
  203.4 1.0 copy-done.12
  204.4 0.9 copy.25
  205.3 2.7 reshape.96
  208.0 1.5 copy.21
  209.5 1.4 slice_reduce_fusion
  210.8 4.1 convolution_convert_fusion.1.refs_1_
  214.9 3.9 convolution_convert_fusion.2.refs_0_
  220.0 2.9 collective-permute-start.3
  222.9 0.7 collective-permute-done.3
  224.3 3.4 fusion.8.refs_3_
  227.7 37.3 %gather.10 = (bf16[8,96,768]{2,1,0:T(8,128)(2,1)}, bf16[8,96,768]{2,1,0:T(8,128)(2,1)}, bf16[4,1152,128]{2,1,0:T(8,128)(2,1)}, bf16[384,1536]{1,0:T(8,128)(2,1)}) custom-call(bf16[96,768]{1,0:T(8,128)(2,1)} %convolution_convert_fusion.2.refs_0_, bf16[96,768]{1,0:T(8,128)(2,1)} %convolution_convert_fusion.1.refs_1_, bf16[1152,128]{1,0:T(8,128)(2,1)} %bitcast.97, ...), custom_call_target="tpu_custom_call" | custom-call | tf_op jit(solution)/shard_map/gather/pallas_call | solution.py:180
  265.0 2.5 fusion.32
  267.5 4.1 fusion.28
  271.7 1.1 copy-done.10
  272.9 2.9 multiply_convert_fusion
  276.0 0.5 collective-permute-start.7
  276.5 8.9 %collective-permute-done.7 = f32[96,1,768]{2,0,1:T(8,128)S(1)} collective-permute-done((f32[96,1,768]{2,0,1:T(8,128)S(1)}, f32[96,1,768]{2,0,1:T(8,128)S(1)}, u32[]{:S(2)}, u32[]{:S(2)}) %collective-permute-start.7) | collective-permute-done | bytes 294944 | tf_op jit(solution)/shard_map/ppermute | solution.py:207
  285.5 0.7 fusion.37.refs_1_
  286.2 1.1 fusion.4
  287.3 2.4 fusion.65
  289.7 71.0 %gather.11 = (bf16[8,384,768]{2,1,0:T(8,128)(2,1)}, bf16[8,96,768]{2,1,0:T(8,128)(2,1)}) custom-call(bf16[384,768]{1,0:T(8,128)(2,1)} %get-tuple-element.65.refs_0_, bf16[96,768]{1,0:T(8,128)(2,1)} %fusion.37.refs_1_), custom_call_target="tpu_custom_call" | custom-call | tf_op jit(solution)/shard_map/gather/pallas_call | solution.py:180
  360.7 4.5 %fusion.70 = f32[384,3072]{1,0:T(8,128)S(1)} fusion(bf16[384,768]{1,0:T(8,128)(2,1)} %get-tuple-element.65.refs_0_, bf16[3072,768]{1,0:T(8,128)(2,1)} %bitcast.100), kind=kOutput, calls=%fused_computation.87 | convolution fusion | flops 1811939328 | bytes 10027008 | tf_op jit(solution)/shard_map/dot_general | solution.py:16
  365.3 2.1 copy-done.1
  367.4 1.2 dynamic-slice_convert_fusion
  368.6 2.7 reshape.101
  371.3 1.5 copy.22
  372.8 4.8 %multiply_reduce_fusion = (f32[]{:T(128)}, f32[768,768]{1,0:T(8,128)}) fusion(bf16[768,768]{0,1:T(8,128)(2,1)} %bitcast.93, bf16[768,768]{0,1:T(8,128)(2,1)} %bitcast.81), kind=kOutput, calls=%fused_computation.6 | convolution fusion | flops 907149312 | bytes 4718596 | tf_op jit(solution)/shard_map/dot_general | solution.py:16
  378.3 2.0 fusion.9
  380.5 7.7 %fusion.66 = (bf16[768,768]{1,0:T(8,128)(2,1)}, f32[768,768]{1,0:T(8,128)}) fusion(f32[768,768]{1,0:T(8,128)} %get-tuple-element.68, f32[]{:T(128)S(6)} %sqrt.11), kind=kOutput, calls=%fused_computation.85 | convolution fusion | flops 1817837568 | bytes 5898244 | tf_op jit(solution)/shard_map/dot_general | solution.py:16
  388.2 2.9 fusion.24
  391.1 2.3 fusion.35
  393.4 15.4 %collective-permute-done.9 = bf16[384,1536]{1,0:T(8,128)(2,1)} collective-permute-done((bf16[384,1536]{1,0:T(8,128)(2,1)S(1)}, bf16[384,1536]{1,0:T(8,128)(2,1)}, u32[]{:S(2)}, u32[]{:S(2)}) %collective-permute-start.9) | collective-permute-done | bytes 1179680 | tf_op jit(solution)/shard_map/ppermute | solution.py:207
  408.8 2.5 add_convert_fusion
  411.4 2.8 collective-permute-done.10
  414.3 2.7 fusion
  417.0 2.1 fusion.17
  (60 shorter events, 0.9 us)
Async XLA Ops:
  2.3 2.2 copy-start.3
  2.3 2.2 copy-start.14
  3.7 43.6 %copy-start.4 = (bf16[96,768]{1,0:T(8,128)(2,1)S(1)}, bf16[96,768]{1,0:T(8,128)(2,1)}, u32[]{:S(2)}) copy-start(bf16[96,768]{1,0:T(8,128)(2,1)} %refs_3_.1) | copy-start | bytes 442372
  49.1 1.3 copy-start.2
  49.8 37.3 %copy-start.7 = (f32[384,768]{1,0:T(8,128)S(1)}, f32[384,768]{1,0:T(8,128)}, u32[]{:S(2)}) copy-start(f32[384,768]{1,0:T(8,128)} %param.11) | copy-start | bytes 3538948
  49.8 41.7 %collective-permute-start = (f32[96,2,192]{2,0,1:T(8,128)S(1)}, f32[96,2,192]{2,0,1:T(8,128)S(1)}, u32[]{:S(2)}, u32[]{:S(2)}) collective-permute-start(f32[96,2,192]{2,0,1:T(8,128)S(1)} %bitcast.99), channel_id=1, source_target_pairs={{0,1},{1,0},{2,3},{3,2},{4,5},{5,4},{6,7},{7,6},{8,9},{9,8},{10,11... | collective-permute-start | bytes 442376 | tf_op jit(solution)/shard_map/ppermute | solution.py:207
  87.1 3.1 copy-start.5
  90.2 2.6 copy-start.6
  91.6 4.7 %collective-permute-start.1 = (f32[96,1,192]{2,0,1:T(8,128)S(1)}, f32[96,1,192]{2,0,1:T(8,128)S(1)}, u32[]{:S(2)}, u32[]{:S(2)}) collective-permute-start(f32[96,1,192]{2,0,1:T(8,128)S(1)} %constant_dynamic-slice_fusion.2), channel_id=1, source_target_pairs={{0,2},{1,3},{2,0},{3,1},{4,6},{5,7},{6,4},{7,5},{8,10},{9,11},{10,... | collective-permute-start | bytes 221192 | tf_op jit(solution)/shard_map/ppermute | solution.py:207
  92.8 3.5 copy-start.16
  200.0 2.2 copy-start
  202.2 1.2 copy-start.13
  203.3 1.1 copy-start.12
  203.3 21.0 %collective-permute-start.4 = (bf16[384,1536]{1,0:T(8,128)(2,1)}, bf16[384,1536]{1,0:T(8,128)(2,1)}, u32[]{:S(2)}, u32[]{:S(2)}) collective-permute-start(bf16[384,1536]{1,0:T(8,128)(2,1)} %dynamic-slice_convert_fusion.1), channel_id=1, source_target_pairs={{0,1},{1,0},{2,3},{3,2},{4,5},{5,4},{6,7},{7,6},{8,9},{9,8},{10,11... | collective-permute-start | bytes 3538952 | tf_op jit(solution)/shard_map/ppermute | solution.py:207
  210.8 8.0 %collective-permute-start.2 = (f32[]{:T(128)}, f32[]{:T(128)}, u32[]{:S(2)}, u32[]{:S(2)}) collective-permute-start(f32[]{:T(128)} %slice_reduce_fusion), channel_id=1, source_target_pairs={{0,1},{1,0},{2,3},{3,2},{4,5},{5,4},{6,7},{7,6},{8,9},{9,8},{10,11... | collective-permute-start | bytes 20 | tf_op jit(solution)/shard_map/ppermute | solution.py:207
  220.0 3.6 collective-permute-start.3
  227.7 37.3 %copy-start.15 = (f32[96,768]{1,0:T(8,128)S(1)}, f32[96,768]{1,0:T(8,128)}, u32[]{:S(2)}) copy-start(f32[96,768]{1,0:T(8,128)} %param.9) | copy-start | bytes 884740
  265.0 2.5 copy-start.11
  271.6 1.3 copy-start.10
  271.6 4.2 %collective-permute-start.6 = (f32[96,2,768]{2,0,1:T(8,128)S(1)}, f32[96,2,768]{2,0,1:T(8,128)S(1)}, u32[]{:S(2)}, u32[]{:S(2)}) collective-permute-start(f32[96,2,768]{2,0,1:T(8,128)S(1)} %dynamic-slice_bitcast_fusion), channel_id=1, source_target_pairs={{0,1},{1,0},{2,3},{3,2},{4,5},{5,4},{6,7},{7,6},{8,9},{9,8},{10,11... | collective-permute-start | bytes 1769480 | tf_op jit(solution)/shard_map/ppermute | solution.py:207
  271.7 14.4 %slice-start = ((s8[4718592]{0:T(1024)(128)(4,1)}), s8[4194304]{0:T(1024)(128)(4,1)S(1)}, s32[]{:S(2)}) async-start(s8[4718592]{0:T(1024)(128)(4,1)} %bitcast.89), calls=%async_computation | async-start | bytes 8388608
  272.8 13.3 %slice-start.1 = ((s8[4718592]{0:T(1024)(128)(4,1)}), s8[524288]{0:T(1024)(128)(4,1)S(1)}, s32[]{:S(2)}) async-start(s8[4718592]{0:T(1024)(128)(4,1)} %bitcast.89), calls=%async_computation.1 | async-start | bytes 1048576
  275.8 10.4 %collective-permute-start.5 = (bf16[384,1536]{1,0:T(8,128)(2,1)S(1)}, bf16[384,1536]{1,0:T(8,128)(2,1)S(1)}, u32[]{:S(2)}, u32[]{:S(2)}) collective-permute-start(bf16[384,1536]{1,0:T(8,128)(2,1)S(1)} %multiply_convert_fusion), channel_id=1, source_target_pairs={{0,1},{1,0},{2,3},{3,2},{4,5},{5,4},{6,7},{7,6},{8,9},{9,8},{10,11... | collective-permute-start | bytes 3538952 | tf_op jit(solution)/shard_map/ppermute | solution.py:207
  276.0 9.5 %collective-permute-start.7 = (f32[96,1,768]{2,0,1:T(8,128)S(1)}, f32[96,1,768]{2,0,1:T(8,128)S(1)}, u32[]{:S(2)}, u32[]{:S(2)}) collective-permute-start(f32[96,1,768]{2,0,1:T(8,128)S(1)} %constant_dynamic-slice_fusion), channel_id=1, source_target_pairs={{0,2},{1,3},{2,0},{3,1},{4,6},{5,7},{6,4},{7,5},{8,10},{9,11},{10,... | collective-permute-start | bytes 884744 | tf_op jit(solution)/shard_map/ppermute | solution.py:207
  365.2 2.2 copy-start.1
  368.6 9.6 %collective-permute-start.8 = (bf16[384,1536]{1,0:T(8,128)(2,1)}, bf16[384,1536]{1,0:T(8,128)(2,1)S(1)}, u32[]{:S(2)}, u32[]{:S(2)}) collective-permute-start(bf16[384,1536]{1,0:T(8,128)(2,1)} %dynamic-slice_convert_fusion), channel_id=1, source_target_pairs={{0,1},{1,0},{2,3},{3,2},{4,5},{5,4},{6,7},{7,6},{8,9},{9,8},{10,11... | collective-permute-start | bytes 3538952 | tf_op jit(solution)/shard_map/ppermute | solution.py:207
  380.3 28.6 %collective-permute-start.9 = (bf16[384,1536]{1,0:T(8,128)(2,1)S(1)}, bf16[384,1536]{1,0:T(8,128)(2,1)}, u32[]{:S(2)}, u32[]{:S(2)}) collective-permute-start(bf16[384,1536]{1,0:T(8,128)(2,1)S(1)} %fusion.9), channel_id=1, source_target_pairs={{0,2},{1,3},{2,0},{3,1},{4,6},{5,7},{6,4},{7,5},{8,10},{9,11},{10,... | collective-permute-start | bytes 3538952 | tf_op jit(solution)/shard_map/ppermute | solution.py:207
  388.2 2.9 copy-start.8
  391.1 25.9 %slice-start.2 = ((s8[4718592]{0:T(1024)(128)(4,1)}), s8[4194304]{0:T(1024)(128)(4,1)S(1)}, s32[]{:S(2)}) async-start(s8[4718592]{0:T(1024)(128)(4,1)} %bitcast.102), calls=%async_computation.2 | async-start | bytes 8388608
  393.4 23.6 %slice-start.3 = ((s8[4718592]{0:T(1024)(128)(4,1)}), s8[524288]{0:T(1024)(128)(4,1)S(1)}, s32[]{:S(2)}) async-start(s8[4718592]{0:T(1024)(128)(4,1)} %bitcast.102), calls=%async_computation.3 | async-start | bytes 1048576
  411.3 5.7 %copy-start.9 = (f32[384,768]{1,0:T(8,128)S(1)}, f32[384,768]{1,0:T(8,128)}, u32[]{:S(2)}) copy-start(f32[384,768]{1,0:T(8,128)} %get-tuple-element.66) | copy-start | bytes 3538948
  411.3 2.9 collective-permute-start.10
where the time goes:
time: 420 us; the launch traced here: 419 us
  Pallas kernels  271 us (65%)
  matrix products  60.3 us (14%)
  local copies, waits for them, and re-layouts  32 us (8%)
  waiting for transfers between devices  30.1 us (7%)
  other arithmetic  16.7 us (4%)
  starting transfers between devices  5.14 us (1%)
    pallas_call x6, Pallas kernels, gather(): pl.pallas_call(functools.partial(gather_kernel, n_shard // 2, n_tensor, l...  271 us
    dot_general x17, matrix products, dot(): lax.dot_general(a, b, (((ca,), (cb,)), ((), ())), preferred_element_type=...  60.3 us
    ppermute x11, waiting for transfers between devices, swap(): lax.ppermute(array, 'tensor', [(i, i ^ bit) for i in range(n_tensor)])  30.1 us
    unnamed x44, local copies, waits for them, and re-layouts  9.47 us
  transfers between devices with their start and end apart: 11, of which 5 were waited for; matrix products, arithmetic and copies ran while one was open for 11% of the time, Pallas kernels for 9%

commit v1 on v0

--- a/solution.py
+++ b/solution.py
@@ -26,6 +26,13 @@
 
 def later_rows(rows, n_chain):
     return rows // (2 * (n_chain - 1)) // 16 * 16
+
+
+def chunks(rows):
+    count = 4 if rows >= 256 else 2
+    units = rows // 16
+    sizes = [(units // count + (k < units % count)) * 16 for k in range(count)]
+    return [size for size in sizes if size] if rows % 16 == 0 else [rows]
 
 
 def gather_kernel(n_chain, n_tensor, n_across, n_along, n_swap, pieces, *refs):
@@ -168,9 +175,13 @@
     pieces = []
     for i, x in enumerate(across):
         later = later_rows(x.shape[0], n_shard // 2)
-        pieces.append((i, 0, x.shape[0] - later, False))
+        main = x.shape[0] - later
+        first = 0
+        for rows in chunks(main) if later else [main]:
+            pieces.append((i, first, rows, False))
+            first += rows
         if later:
-            pieces.append((i, x.shape[0] - later, later, True))
+            pieces.append((i, main, later, True))
     shapes = [(n_shard, *x.shape) for x in across]
     shapes += [(n_tensor, *x.shape) for x in along] + [x.shape for x in swaps]
     counts = [(n_shard + 3, n_shard)] * len(pieces) + [(3, n_tensor)] * len(along) + [(1, 1)] * len(swaps)
@@ -207,11 +218,11 @@
     return lax.ppermute(array, "tensor", [(i, i ^ bit) for i in range(n_tensor)])
 
 
-def gram_half(parts, core, n_tensor):
-    half = parts.shape[1] // 2
-    mine = part(parts, core, half, 1)
-    other = part(parts, 1 - core, half, 1)
-    return mine + swap(other.astype(BF16), 1, n_tensor).astype(F32)
+def gram_half(rows, panel, core, n_tensor):
+    half = panel.shape[0] // 2
+    other = dot(rows, part(panel, 1 - core, half, 0), 1, 1).astype(BF16)
+    other = swap(other, 1, n_tensor)
+    return dot(rows, part(panel, core, half, 0), 1, 1) + other.astype(F32)
 
 
 def apply_gram(halves, panel, core):
@@ -268,31 +279,32 @@
         first = s * rows_right
         owner = first // block_hidden
         strip = lax.dynamic_slice_in_dim(panel, first - owner * block_hidden, rows_right, 1)
-        right_1, strips, left = run(1, [thirds[1]], [strip, lanes(left_blocks.reshape(-1, block_left))])
-        left = side_by_side(left.reshape(n_tensor, n_shard * rows_left, block_left))
+        right_1, strips = run(1, [thirds[1]], [strip])
         strip = pick(strips, owner, 0)
         stat_right_new = 0.95 * stat_right + 0.05 * dot(strip, panel, 0, 0)
         cross_left = scatter_sum(dot(gradient, panel, 1, 1), t, n_tensor)
         stat_left_new = 0.95 * stat_left + 0.05 * cross_left
-        right_2, stat_left_columns, stat_right_rows = run(
-            2, [thirds[2], lanes(stat_left_new.astype(BF16))], [stat_right_new.astype(BF16)]
+        right_2, stat_left_columns, stat_right_rows, left = run(
+            2,
+            [thirds[2], lanes(stat_left_new.astype(BF16))],
+            [stat_right_new.astype(BF16), lanes(left_blocks.reshape(-1, block_left))],
         )
+        left = side_by_side(left.reshape(n_tensor, n_shard * rows_left, block_left))
         right_columns = stacked(jnp.concatenate([right_0, right_1, right_2], axis=1))
 
         power = dot(side_by_side(stat_right_rows), right_columns, 1, 0)
         power_half = power.astype(BF16)
         square = jnp.full((8, 128), jnp.sum(power * power), F32)
-        grad_right = dot(side_by_side(grad_rows), right_columns, 1, 0).astype(BF16)
-        moment_right = dot(side_by_side(moment_rows), right_columns, 1, 0).astype(BF16)
+        rotated = jnp.concatenate([side_by_side(grad_rows), side_by_side(moment_rows)])
+        rotated = dot(rotated, right_columns, 1, 0).astype(BF16)
+        grad_right, moment_right = rotated[:rows_left], rotated[rows_left:]
         power_panel, squares = run(3, [power_half, square], [])
         power_panel = stacked(power_panel)
 
         square = whole_sum(jnp.sum(squares[:, 0, 0]), n_tensor)
         scale = 1.0 / jnp.sqrt(square + 1e-06)
-        mine = gram_half(dot(power_half, power_panel, 1, 1), core, n_tensor)
-        grad_right, moment_right, stat_left_all, there = run(
-            4, [grad_right, moment_right], [lanes(stat_left_columns.reshape(-1, 128))], [mine.astype(BF16)]
-        )
+        mine = gram_half(power_half, power_panel, core, n_tensor)
+        grad_right, moment_right, there = run(4, [grad_right, moment_right], [], [mine.astype(BF16)])
         mine = (((mine + there.astype(F32)) * scale) * scale).astype(BF16)
         halves = mine, swap(mine, 1, n_tensor)
         iterate = scale * (1.5 * power - 0.5 * apply_gram(halves, power_panel, core))
@@ -304,7 +316,7 @@
         scaled = (moment_turned / (jnp.sqrt(second_new) + 1e-08)).astype(BF16)
         back_half = scatter_sum(dot(scaled, right_columns, 1, 1), t, n_tensor).astype(BF16)
 
-        def left_basis():
+        def left_basis(stat_left_all):
             stat_all = side_by_side(stat_left_all.reshape(n_tensor, n_shard * rows_left, block_left))
             power_left = dot(stat_all, left, 1, 0)
             iterate_left = power_left / jnp.sqrt(jnp.sum(power_left * power_left) + 1e-06)
@@ -319,21 +331,35 @@
                     iterate_left = 1.5 * own - 0.5 * dot(gram, part(left_half, t, block_left, 1), 1, 0)
             return iterate_left
 
+        def gram_whole(mine, there):
+            mine = (mine + there.astype(F32)).astype(BF16)
+            return mine, swap(mine, 1, n_tensor)
+
         update = None
         for step in range(NS_ITERS - 1):
             iterate_half = iterate.astype(BF16)
-            sent = [iterate_half] + ([back_half] if step == 0 else [])
-            gathered = run(5 + step, sent, [])
-            iterate_panel = stacked(gathered[0])
+            upper, lower = jnp.split(iterate_half, 2)
+            (upper,) = run(5 + 2 * step, [upper], [])
+            upper = stacked(upper)
+            mine_upper = gram_half(iterate_half, upper, core, n_tensor)
             if step == 0:
-                update = dot(part(left, s, rows_left, 0), stacked(gathered[1]), 1, 0)
-            mine = gram_half(dot(iterate_half, iterate_panel, 1, 1), core, n_tensor)
-            there = swap(mine.astype(BF16), n_tensor // 2, n_tensor)
+                lower, back_panel, stat_left_all, there_upper = run(
+                    6, [lower, back_half], [lanes(stat_left_columns.reshape(-1, 128))], [mine_upper.astype(BF16)]
+                )
+                update = dot(part(left, s, rows_left, 0), stacked(back_panel), 1, 0)
+            else:
+                lower, there_upper = run(6 + 2 * step, [lower], [], [mine_upper.astype(BF16)])
+            lower = stacked(lower)
+            mine_lower = gram_half(iterate_half, lower, core, n_tensor)
+            there_lower = swap(mine_lower.astype(BF16), n_tensor // 2, n_tensor)
+            halves = gram_whole(mine_upper, there_upper)
+            change = apply_gram(halves, upper, core)
             if step == NS_ITERS - 2:
-                there, iterate_left, update = lax.optimization_barrier((there, left_basis(), update))
-            mine = (mine + there.astype(F32)).astype(BF16)
-            halves = mine, swap(mine, 1, n_tensor)
-            iterate = 1.5 * iterate - 0.5 * apply_gram(halves, iterate_panel, core)
+                there_lower, iterate_left, update, change = lax.optimization_barrier(
+                    (there_lower, left_basis(stat_left_all), update, change)
+                )
+            change = change + apply_gram(gram_whole(mine_lower, there_lower), lower, core)
+            iterate = 1.5 * iterate - 0.5 * change
 
         return (
             update,

time: 420 us -> 407 us (0.969)
  Pallas kernels: 271 us -> 261 us
  matrix products: 60.3 us -> 70.2 us
  waiting for transfers between devices: 30.1 us -> 24.5 us
  other arithmetic: 16.7 us -> 11.7 us
  local copies, waits for them, and re-layouts: 32 us -> 27.3 us
    pallas_call x6 -> x7, Pallas kernels: 271 us -> 261 us  [gather(): pl.pallas_call(functools.partial(gather_kernel, n_shard // 2, n_tensor, l...]
    dot_general x17 -> x22, matrix products: 60.3 us -> 70.2 us  [dot(): lax.dot_general(a, b, (((ca,), (cb,)), ((), ())), preferred_element_type=...]
    convert_element_type x3 -> x2, other arithmetic: 7.88 us -> 1.64 us  [gram_whole(): mine = (mine + there.astype(F32)).astype(BF16)]
    ppermute x11 -> x13, waiting for transfers between devices: 30.1 us -> 24.5 us  [swap(): lax.ppermute(array, 'tensor', [(i, i ^ bit) for i in range(n_tensor)])]
    unnamed x44 -> x50, local copies, waits for them, and re-layouts: 9.47 us -> 4.62 us
  transfers between devices with their start and end apart: 11 -> 13, of which waited for: 5 -> 6; matrix products, arithmetic and copies ran while one was open for 11% -> 14% of each run, Pallas kernels for 9% -> 7%
where the time goes in v1:
time: 407 us; the launch traced here: 406 us
  Pallas kernels  261 us (64%)
  matrix products  70.2 us (17%)
  local copies, waits for them, and re-layouts  27.3 us (7%)
  waiting for transfers between devices  24.5 us (6%)
  other arithmetic  11.7 us (3%)
  starting transfers between devices  7.64 us (2%)
    pallas_call x7, Pallas kernels, gather(): pl.pallas_call(functools.partial(gather_kernel, n_shard // 2, n_tensor, l...  261 us
    dot_general x22, matrix products, dot(): lax.dot_general(a, b, (((ca,), (cb,)), ((), ())), preferred_element_type=...  70.2 us
    ppermute x13, waiting for transfers between devices, swap(): lax.ppermute(array, 'tensor', [(i, i ^ bit) for i in range(n_tensor)])  24.5 us
  transfers between devices with their start and end apart: 13, of which 6 were waited for; matrix products, arithmetic and copies ran while one was open for 14% of the time, Pallas kernels for 7%

profile of v1, /device:TPU:0, one launch (start us, length us, event | category | flops | bytes accessed | tf_op | source)
XLA Modules:
  0.0 405.9 jit_solution(6740668072379392922)
XLA Ops:
  0.7 1.4 convert.5
  2.1 0.8 fusion.82
  2.9 0.7 reshape.89.refs_1_
  3.7 0.8 fusion.80
  4.5 40.9 %gather.7 = (bf16[8,96,768]{2,1,0:T(8,128)(2,1)}, bf16[8,144,128]{2,1,0:T(8,128)(2,1)}, bf16[8,128,768]{2,1,0:T(8,128)(2,1)}, bf16[4,96,768]{2,1,0:T(8,128)(2,1)}, bf16[4,96,768]{2,1,0:T(8,128)(2,1)}) custom-call(bf16[96,768]{1,0:T(8,128)(2,1)} %refs_3_.1, bf16[144,128]{1,0:T(8,128)(2,1)} %reshape.89.refs_1_, bf16[128,768]{1,0:T(8,128)(2,1)} %get-tuple-element.64.refs_2_, ...), custom_call_target="tpu_custom_call" | custom-call | tf_op jit(solution)/shard_map/gather/pallas_call | solution.py:191
  45.4 1.8 convolution_bitcast_fusion
  48.4 0.9 constant_dynamic-slice_fusion.1.refs_1_
  49.3 27.2 %gather.8 = (bf16[8,128,768]{2,1,0:T(8,128)(2,1)}, bf16[4,768,384]{2,1,0:T(8,128)(2,1)}) custom-call(bf16[128,768]{1,0:T(8,128)(2,1)} %get-tuple-element.63.refs_0_, bf16[768,384]{1,0:T(8,128)(2,1)} %constant_dynamic-slice_fusion.1.refs_1_), custom_call_target="tpu_custom_call" | custom-call | tf_op jit(solution)/shard_map/gather/pallas_call | solution.py:191
  76.5 3.1 fusion.84
  79.6 1.3 constant_dynamic-update-slice_fusion.2
  80.9 1.7 collective-permute-start.1
  82.6 1.3 constant_dynamic-update-slice_fusion.1
  83.9 1.7 collective-permute-done.1
  85.6 0.7 fusion.79
  86.3 0.7 reshape.92.refs_1_
  87.0 38.3 %gather.9 = (bf16[8,128,768]{2,1,0:T(8,128)(2,1)}, bf16[8,144,128]{2,1,0:T(8,128)(2,1)}, bf16[4,384,768]{2,1,0:T(8,128)(2,1)}, bf16[4,1152,128]{2,1,0:T(8,128)(2,1)}) custom-call(bf16[128,768]{1,0:T(8,128)(2,1)} %get-tuple-element.65.refs_0_, bf16[144,128]{1,0:T(8,128)(2,1)} %reshape.92.refs_1_, bf16[384,768]{1,0:T(8,128)(2,1)} %get-tuple-element.70.refs_2_, ...), custom_call_target="tpu_custom_call" | custom-call | tf_op jit(solution)/shard_map/gather/pallas_call | solution.py:191
  125.3 3.0 copy.18
  128.3 2.7 constant_dynamic-update-slice_fusion
  131.0 6.2 %multiply_reduce_fusion.1 = (f32[]{:T(128)}, bf16[384,768]{1,0:T(8,128)(2,1)}, f32[384,768]{1,0:T(8,128)}) fusion(bf16[384,3072]{0,1:T(8,128)(2,1)S(1)} %bitcast.75, bf16[3072,768]{1,0:T(8,128)(2,1)} %bitcast.9), kind=kOutput, calls=%fused_computation.30 | convolution fusion | flops 1812824064 | bytes 8847364 | tf_op jit(solution)/shard_map/dot_general | solution.py:16
  137.2 1.2 broadcast_in_dim.3.refs_1_
  138.5 51.2 %gather.10 = (bf16[8,384,768]{2,1,0:T(8,128)(2,1)}, f32[8,8,128]{2,1,0:T(8,128)}) custom-call(bf16[384,768]{1,0:T(8,128)(2,1)} %get-tuple-element.60.refs_0_, f32[8,128]{1,0:T(8,128)} %broadcast_in_dim.3.refs_1_), custom_call_target="tpu_custom_call" | custom-call | tf_op jit(solution)/shard_map/gather/pallas_call | solution.py:191
  189.7 4.1 %convolution_convert_fusion = bf16[384,1536]{1,0:T(8,128)(2,1)} fusion(bf16[384,768]{1,0:T(8,128)(2,1)} %get-tuple-element.60.refs_0_, bf16[3072,768]{1,0:T(8,128)(2,1)} %bitcast.85, s32[]{:T(128)S(6)} %select_n.99), kind=kOutput, calls=%fused_computation | convolution fusion | flops 906559488 | bytes 4128772 | tf_op jit(solution)/shard_map/dot_general | solution.py:16
  193.8 1.0 copy-done.17
  194.8 0.9 copy.25
  195.7 1.4 slice_reduce_fusion
  197.1 0.9 reshape.98
  198.0 1.5 copy.21
  199.5 3.5 convolution_convert_fusion.4
  203.0 0.7 fusion.83
  205.0 2.8 collective-permute-start.3
  207.8 0.9 collective-permute-done.3
  209.4 4.1 %fusion.85 = (bf16[384,1536]{1,0:T(8,128)(2,1)}, f32[384,1536]{1,0:T(8,128)S(1)}) fusion(bf16[384,1536]{1,0:T(8,128)(2,1)} %collective-permute-done.4, bf16[384,768]{1,0:T(8,128)(2,1)S(1)} %copy-done.2, bf16[3072,768]{1,0:T(8,128)(2,1)} %bitcast.86, s32[]{:T(128)S(6)} %select_n.98), kind=kOutput, calls=%fused_computation.109 | convolution fusion | flops 907739136 | bytes 7667716 | tf_op jit(solution)/shard_map/dot_general | solution.py:16
  213.5 30.4 %gather.11 = (bf16[8,96,768]{2,1,0:T(8,128)(2,1)}, bf16[8,96,768]{2,1,0:T(8,128)(2,1)}, bf16[384,1536]{1,0:T(8,128)(2,1)}) custom-call(bf16[96,768]{1,0:T(8,128)(2,1)} %get-tuple-element.69.refs_0_, bf16[96,768]{1,0:T(8,128)(2,1)} %get-tuple-element.68.refs_1_, bf16[384,1536]{1,0:T(8,128)(2,1)} %get-tuple-element.73.refs_2_), custom_call_target="tpu_custom_call" | custom-call | tf_op jit(solution)/shard_map/gather/pallas_call | solution.py:191
  244.0 1.8 multiply_convert_fusion
  245.9 2.5 fusion.41
  248.3 4.1 %fusion.37 = f32[96,2,2,768]{3,0,2,1:T(8,128)S(1)} fusion(bf16[2,2,768,768]{3,2,1,0:T(8,128)(2,1)} %bitcast.19, bf16[768,768]{1,0:T(8,128)(2,1)S(1)} %bitcast.101, f32[96,768]{1,0:T(8,128)} %fusion.41, bf16[768,768]{0,1:T(8,128)(2,1)} %bitcast.90, s32[]{:T(128)S(6)} %select_n.100), kind=kOutput, calls=%fused_computation.52 | convolution fusion | flops 566452224 | bytes 7520260 | tf_op jit(solution)/shard_map/dot_general | solution.py:16
  252.6 2.1 collective-permute-done.6
  254.7 1.1 bitcast_add_fusion
  255.9 3.3 fusion
  259.1 3.8 fusion.86
  263.0 0.9 fusion.81
  263.8 31.9 %gather.12 = bf16[8,192,768]{2,1,0:T(8,128)(2,1)} custom-call(bf16[192,768]{1,0:T(8,128)(2,1)} %get-tuple-element.61.refs_0_), custom_call_target="tpu_custom_call" | custom-call | tf_op jit(solution)/shard_map/gather/pallas_call | solution.py:191
  295.8 2.9 convolution_convert_fusion.3
  298.7 0.7 constant_dynamic-slice_fusion
  299.4 0.7 collective-permute-start.7
  300.0 9.1 %collective-permute-done.7 = f32[96,1,768]{2,0,1:T(8,128)} collective-permute-done((f32[96,1,768]{2,0,1:T(8,128)}, f32[96,1,768]{2,0,1:T(8,128)}, u32[]{:S(2)}, u32[]{:S(2)}) %collective-permute-start.7) | collective-permute-done | bytes 294944 | tf_op jit(solution)/shard_map/ppermute | solution.py:218
  309.1 1.7 fusion.46.refs_1_
  310.8 2.9 fusion.87
  313.7 41.0 %gather.13 = (bf16[8,192,768]{2,1,0:T(8,128)(2,1)}, bf16[8,96,768]{2,1,0:T(8,128)(2,1)}, bf16[4,1152,128]{2,1,0:T(8,128)(2,1)}, bf16[384,768]{1,0:T(8,128)(2,1)}) custom-call(bf16[192,768]{1,0:T(8,128)(2,1)} %get-tuple-element.62.refs_0_, bf16[96,768]{1,0:T(8,128)(2,1)} %fusion.46.refs_1_, bf16[1152,128]{1,0:T(8,128)(2,1)} %bitcast.106, ...), custom_call_target="tpu_custom_call" | custom-call | tf_op jit(solution)/shard_map/gather/pallas_call | solution.py:191
  354.7 1.5 add_convert_fusion.1
  356.3 3.6 reshape.105
  359.9 2.5 copy.22
  362.4 4.8 %multiply_reduce_fusion = (f32[]{:T(128)}, f32[768,768]{1,0:T(8,128)}) fusion(bf16[768,768]{0,1:T(8,128)(2,1)} %bitcast.100, bf16[768,768]{0,1:T(8,128)(2,1)} %bitcast.91), kind=kOutput, calls=%fused_computation.2 | convolution fusion | flops 907149312 | bytes 4718596 | tf_op jit(solution)/shard_map/dot_general | solution.py:16
  367.9 2.8 convolution_convert_fusion.2
  371.2 8.1 %fusion.89 = (bf16[768,768]{1,0:T(8,128)(2,1)}, f32[768,768]{1,0:T(8,128)}) fusion(f32[768,768]{1,0:T(8,128)} %get-tuple-element.82, f32[]{:T(128)S(6)} %sqrt.11), kind=kOutput, calls=%fused_computation.113 | convolution fusion | flops 1817837568 | bytes 5898244 | tf_op jit(solution)/shard_map/dot_general | solution.py:16
  379.2 2.5 fusion.44
  381.8 3.4 fusion.88
  385.1 1.7 collective-permute-start.10
  386.8 2.8 fusion.17
  389.6 1.7 fusion.26
  392.0 8.7 %collective-permute-done.10 = bf16[384,768]{1,0:T(8,128)(2,1)S(1)} collective-permute-done((bf16[384,768]{1,0:T(8,128)(2,1)}, bf16[384,768]{1,0:T(8,128)(2,1)S(1)}, u32[]{:S(2)}, u32[]{:S(2)}) %collective-permute-start.10) | collective-permute-done | bytes 589856 | tf_op jit(solution)/shard_map/ppermute | solution.py:218
  400.8 2.0 collective-permute-done.12
  403.4 0.6 convolution_add_fusion
  404.7 1.2 multiply_subtract_fusion.1
  (74 shorter events, 4.2 us)
Async XLA Ops:
  0.7 2.3 copy-start.22
  0.7 3.0 copy-start.8
  0.7 3.0 copy-start.20
  2.9 42.4 %copy-start.9 = (bf16[96,768]{1,0:T(8,128)(2,1)S(1)}, bf16[96,768]{1,0:T(8,128)(2,1)}, u32[]{:S(2)}) copy-start(bf16[96,768]{1,0:T(8,128)(2,1)} %refs_3_.1) | copy-start | bytes 442372
  47.1 1.3 copy-start.1
  47.9 28.6 %copy-start.13 = (f32[384,768]{1,0:T(8,128)S(1)}, f32[384,768]{1,0:T(8,128)}, u32[]{:S(2)}) copy-start(f32[384,768]{1,0:T(8,128)} %param.11) | copy-start | bytes 3538948
  47.9 33.0 %collective-permute-start = (f32[96,2,192]{2,0,1:T(8,128)S(1)}, f32[96,2,192]{2,0,1:T(8,128)S(1)}, u32[]{:S(2)}, u32[]{:S(2)}) collective-permute-start(f32[96,2,192]{2,0,1:T(8,128)S(1)} %bitcast.108), channel_id=1, source_target_pairs={{0,1},{1,0},{2,3},{3,2},{4,5},{5,4},{6,7},{7,6},{8,9},{9,8},{10,11... | collective-permute-start | bytes 442376 | tf_op jit(solution)/shard_map/ppermute | solution.py:218
  76.5 3.1 copy-start.11
  79.6 3.0 copy-start.12
  80.9 4.7 %collective-permute-start.1 = (f32[96,1,192]{2,0,1:T(8,128)S(1)}, f32[96,1,192]{2,0,1:T(8,128)S(1)}, u32[]{:S(2)}, u32[]{:S(2)}) collective-permute-start(f32[96,1,192]{2,0,1:T(8,128)S(1)} %constant_dynamic-slice_fusion.2), channel_id=1, source_target_pairs={{0,2},{1,3},{2,0},{3,1},{4,6},{5,7},{6,4},{7,5},{8,10},{9,11},{10,... | collective-permute-start | bytes 221192 | tf_op jit(solution)/shard_map/ppermute | solution.py:218
  82.6 3.0 copy-start.23
  189.7 4.1 %copy-start.18 = (bf16[4,96,768]{2,1,0:T(8,128)(2,1)S(1)}, bf16[4,96,768]{2,1,0:T(8,128)(2,1)}, u32[]{:S(2)}) copy-start(bf16[4,96,768]{2,1,0:T(8,128)(2,1)} %get-tuple-element.40) | copy-start | bytes 1769476
  193.8 1.1 copy-start.17
  193.8 15.6 %collective-permute-start.4 = (bf16[384,1536]{1,0:T(8,128)(2,1)}, bf16[384,1536]{1,0:T(8,128)(2,1)}, u32[]{:S(2)}, u32[]{:S(2)}) collective-permute-start(bf16[384,1536]{1,0:T(8,128)(2,1)} %convolution_convert_fusion), channel_id=1, source_target_pairs={{0,1},{1,0},{2,3},{3,2},{4,5},{5,4},{6,7},{7,6},{8,9},{9,8},{10,11... | collective-permute-start | bytes 3538952 | tf_op jit(solution)/shard_map/ppermute | solution.py:218
  193.8 3.3 copy-start.15
  197.1 6.7 %collective-permute-start.2 = (f32[]{:T(128)}, f32[]{:T(128)}, u32[]{:S(2)}, u32[]{:S(2)}) collective-permute-start(f32[]{:T(128)} %slice_reduce_fusion), channel_id=1, source_target_pairs={{0,1},{1,0},{2,3},{3,2},{4,5},{5,4},{6,7},{7,6},{8,9},{9,8},{10,11... | collective-permute-start | bytes 20 | tf_op jit(solution)/shard_map/ppermute | solution.py:218
  198.0 1.5 copy-start.19
  199.5 9.9 %copy-start.2 = (bf16[384,768]{1,0:T(8,128)(2,1)S(1)}, bf16[384,768]{1,0:T(8,128)(2,1)}, u32[]{:S(2)}) copy-start(bf16[384,768]{1,0:T(8,128)(2,1)} %get-tuple-element.60.refs_0_) | copy-start | bytes 1769476
  205.0 3.7 collective-permute-start.3
  244.0 1.9 copy-start.14
  244.0 1.9 copy-start.21
  245.8 6.7 %copy-start.4 = (bf16[384,1536]{1,0:T(8,128)(2,1)}, bf16[384,1536]{1,0:T(8,128)(2,1)S(1)}, u32[]{:S(2)}) copy-start(bf16[384,1536]{1,0:T(8,128)(2,1)S(1)} %multiply_convert_fusion) | copy-start | bytes 3538948
  245.8 2.6 copy-start.16
  245.8 10.1 %collective-permute-start.5 = (bf16[384,1536]{1,0:T(8,128)(2,1)S(1)}, bf16[384,1536]{1,0:T(8,128)(2,1)}, u32[]{:S(2)}, u32[]{:S(2)}) collective-permute-start(bf16[384,1536]{1,0:T(8,128)(2,1)S(1)} %multiply_convert_fusion), channel_id=1, source_target_pairs={{0,1},{1,0},{2,3},{3,2},{4,5},{5,4},{6,7},{7,6},{8,9},{9,8},{10,11... | collective-permute-start | bytes 3538952 | tf_op jit(solution)/shard_map/ppermute | solution.py:218
  252.5 2.2 collective-permute-start.6
  255.8 3.3 copy-start.3
  255.8 3.3 copy-start.5
  295.7 15.0 %copy-start = (bf16[8,192,768]{2,1,0:T(8,128)(2,1)S(1)}, bf16[8,192,768]{2,1,0:T(8,128)(2,1)}, u32[]{:S(2)}) copy-start(bf16[8,192,768]{2,1,0:T(8,128)(2,1)} %gather.12) | copy-start | bytes 7077892
  298.6 12.1 %collective-permute-start.8 = (bf16[384,768]{1,0:T(8,128)(2,1)}, bf16[384,768]{1,0:T(8,128)(2,1)}, u32[]{:S(2)}, u32[]{:S(2)}) collective-permute-start(bf16[384,768]{1,0:T(8,128)(2,1)} %convolution_convert_fusion.3), channel_id=1, source_target_pairs={{0,1},{1,0},{2,3},{3,2},{4,5},{5,4},{6,7},{7,6},{8,9},{9,8},{10,11... | collective-permute-start | bytes 1769480 | tf_op jit(solution)/shard_map/ppermute | solution.py:218
  299.4 9.7 %collective-permute-start.7 = (f32[96,1,768]{2,0,1:T(8,128)}, f32[96,1,768]{2,0,1:T(8,128)}, u32[]{:S(2)}, u32[]{:S(2)}) collective-permute-start(f32[96,1,768]{2,0,1:T(8,128)} %constant_dynamic-slice_fusion), channel_id=1, source_target_pairs={{0,2},{1,3},{2,0},{3,1},{4,6},{5,7},{6,4},{7,5},{8,10},{9,11},{10,... | collective-permute-start | bytes 884744 | tf_op jit(solution)/shard_map/ppermute | solution.py:218
  356.2 33.4 %collective-permute-start.11 = (bf16[384,768]{1,0:T(8,128)(2,1)S(1)}, bf16[384,768]{1,0:T(8,128)(2,1)}, u32[]{:S(2)}, u32[]{:S(2)}) collective-permute-start(bf16[384,768]{1,0:T(8,128)(2,1)S(1)} %add_convert_fusion.1), channel_id=1, source_target_pairs={{0,1},{1,0},{2,3},{3,2},{4,5},{5,4},{6,7},{7,6},{8,9},{9,8},{10,11... | collective-permute-start | bytes 1769480 | tf_op jit(solution)/shard_map/ppermute | solution.py:218
  370.7 11.1 %collective-permute-start.9 = (bf16[384,768]{1,0:T(8,128)(2,1)}, bf16[384,768]{1,0:T(8,128)(2,1)}, u32[]{:S(2)}, u32[]{:S(2)}) collective-permute-start(bf16[384,768]{1,0:T(8,128)(2,1)} %convolution_convert_fusion.2), channel_id=1, source_target_pairs={{0,1},{1,0},{2,3},{3,2},{4,5},{5,4},{6,7},{7,6},{8,9},{9,8},{10,11... | collective-permute-start | bytes 1769480 | tf_op jit(solution)/shard_map/ppermute | solution.py:218
  385.1 15.5 %collective-permute-start.10 = (bf16[384,768]{1,0:T(8,128)(2,1)}, bf16[384,768]{1,0:T(8,128)(2,1)S(1)}, u32[]{:S(2)}, u32[]{:S(2)}) collective-permute-start(bf16[384,768]{1,0:T(8,128)(2,1)} %get-tuple-element.79), channel_id=1, source_target_pairs={{0,2},{1,3},{2,0},{3,1},{4,6},{5,7},{6,4},{7,5},{8,10},{9,11},{10,... | collective-permute-start | bytes 1769480 | tf_op jit(solution)/shard_map/ppermute | solution.py:218
  391.3 9.3 %copy-start.6 = (f32[384,768]{1,0:T(8,128)S(1)}, f32[384,768]{1,0:T(8,128)}, u32[]{:S(2)}) copy-start(f32[384,768]{1,0:T(8,128)} %get-tuple-element.80) | copy-start | bytes 3538948
  400.6 2.2 copy-start.10
  400.7 2.1 collective-permute-start.12
  403.4 1.3 copy-start.7

commit v2 on v1

--- a/solution.py
+++ b/solution.py
@@ -35,8 +35,8 @@
     return [size for size in sizes if size] if rows % 16 == 0 else [rows]
 
 
-def gather_kernel(n_chain, n_tensor, n_across, n_along, n_swap, pieces, *refs):
-    count = n_across + n_along + n_swap
+def gather_kernel(n_chain, n_tensor, n_across, n_along, n_swap, n_cast, cast_ratio, pieces, *refs):
+    count = n_across + n_along + n_swap + n_cast
     ins, outs = refs[:count], refs[count : 2 * count]
     local_sem = refs[2 * count]
     sems = refs[2 * count + 1 :]
@@ -48,8 +48,8 @@
     near_t = t + 1 - 2 * (t % 2)
     far_t = lax.rem(t + n_tensor // 2, n_tensor)
     near, far = (s, near_t), (s, far_t)
-    others = ([pair, right, left] if n_across else []) + ([near] if n_along else [])
-    others += [far] if n_along or n_swap else []
+    others = ([pair, right, left] if n_across else []) + ([near] if n_along or n_cast else [])
+    others += [far] if n_along or n_swap or n_cast else []
     barrier = pltpu.get_barrier_semaphore()
     for other in others:
         pl.semaphore_signal(barrier, inc=1, device_id=other, device_id_type=pl.DeviceIdType.MESH)
@@ -80,6 +80,17 @@
     def swap(i):
         pos = 2 * (len(pieces) + i - n_across)
         return remote(ins[i], outs[i], sems[pos].at[0], sems[pos + 1].at[0], far)
+
+    owner = (s * cast_ratio[0]) // cast_ratio[1]
+    is_owner, is_far = t == owner, far_t == owner
+    is_other = (near_t == owner) | (near_t + far_t - t == owner)
+
+    def cast(i, send, target, own=False):
+        pos = 2 * (len(pieces) + i - n_across)
+        return remote(ins[i] if own else outs[i], outs[i], sems[pos].at[send], sems[pos + 1].at[0], target)
+
+    def keep(i):
+        return pltpu.make_async_copy(ins[i], outs[i], local_sem.at[i])
 
     has_right, has_left = a + 1 < n_chain, a >= 1
     extra = 2 * n_chain
@@ -91,8 +102,17 @@
     for i in range(n_across, n_across + n_along):
         along(i, t, 0, far, True).start()
         along(i, t, 1, near, True).start()
-    for i in range(n_across + n_along, count):
+    n_gathered = n_across + n_along
+    for i in range(n_gathered, n_gathered + n_swap):
         swap(i).start()
+    for i in range(n_gathered + n_swap, count):
+
+        @pl.when(is_owner)
+        def _():
+            cast(i, 0, far, True).start()
+            cast(i, 1, near, True).start()
+            keep(i).start()
+
     locals_ = []
     for i in range(n_across + n_along):
         own = pltpu.make_async_copy(ins[i], outs[i].at[s if i < n_across else t], local_sem.at[i])
@@ -136,6 +156,13 @@
     for i in range(n_across, n_across + n_along):
         along(i, far_t, 2, near).wait_recv()
         along(i, far_t, 2, near).start()
+    for i in range(n_gathered + n_swap, count):
+
+        @pl.when(is_far)
+        def _():
+            cast(i, 0, near).wait_recv()
+            cast(i, 0, near).start()
+
     if n_across:
         step(n_chain - 1, 0)
 
@@ -164,14 +191,24 @@
         along(i, near_far, 2, near).wait_recv()
         for send in range(3):
             along(i, t, send, near).wait_send()
-    for i in range(n_across + n_along, count):
+    for i in range(n_gathered, n_gathered + n_swap):
         swap(i).wait()
+    for i in range(n_gathered + n_swap, count):
+        pl.when(is_other)(lambda i=i: cast(i, 0, near).wait_recv())
+        pl.when(is_far)(lambda i=i: cast(i, 0, near).wait_send())
+
+        @pl.when(is_owner)
+        def _():
+            cast(i, 0, far, True).wait_send()
+            cast(i, 1, near, True).wait_send()
+            keep(i).wait()
+
     for own in locals_:
         own.wait()
 
 
-def gather(name, across, along, swaps=(), *, n_shard, n_tensor):
-    arrays = list(across) + list(along) + list(swaps)
+def gather(name, across, along, swaps=(), casts=(), cast_ratio=(0, 1), *, n_shard, n_tensor):
+    arrays = list(across) + list(along) + list(swaps) + list(casts)
     pieces = []
     for i, x in enumerate(across):
         later = later_rows(x.shape[0], n_shard // 2)
@@ -183,14 +220,23 @@
         if later:
             pieces.append((i, main, later, True))
     shapes = [(n_shard, *x.shape) for x in across]
-    shapes += [(n_tensor, *x.shape) for x in along] + [x.shape for x in swaps]
+    shapes += [(n_tensor, *x.shape) for x in along] + [x.shape for x in [*swaps, *casts]]
     counts = [(n_shard + 3, n_shard)] * len(pieces) + [(3, n_tensor)] * len(along) + [(1, 1)] * len(swaps)
+    counts += [(2, 1)] * len(casts)
     scratch = [pltpu.SemaphoreType.DMA((len(arrays),))]
     for sends, receives in counts:
         scratch += [pltpu.SemaphoreType.DMA((sends,)), pltpu.SemaphoreType.DMA((receives,))]
     return pl.pallas_call(
         functools.partial(
-            gather_kernel, n_shard // 2, n_tensor, len(across), len(along), len(swaps), tuple(pieces)
+            gather_kernel,
+            n_shard // 2,
+            n_tensor,
+            len(across),
+            len(along),
+            len(swaps),
+            len(casts),
+            cast_ratio,
+            tuple(pieces),
         ),
         out_shape=[jax.ShapeDtypeStruct(shape, x.dtype) for shape, x in zip(shapes, arrays)],
         in_specs=[pl.BlockSpec(memory_space=pl.ANY)] * len(arrays),
@@ -279,15 +325,18 @@
         first = s * rows_right
         owner = first // block_hidden
         strip = lax.dynamic_slice_in_dim(panel, first - owner * block_hidden, rows_right, 1)
-        right_1, strips = run(1, [thirds[1]], [strip])
-        strip = pick(strips, owner, 0)
+        right_1, left, strip = run(
+            1,
+            [thirds[1]],
+            [lanes(left_blocks.reshape(-1, block_left))],
+            casts=[strip],
+            cast_ratio=(rows_right, block_hidden),
+        )
         stat_right_new = 0.95 * stat_right + 0.05 * dot(strip, panel, 0, 0)
         cross_left = scatter_sum(dot(gradient, panel, 1, 1), t, n_tensor)
         stat_left_new = 0.95 * stat_left + 0.05 * cross_left
-        right_2, stat_left_columns, stat_right_rows, left = run(
-            2,
-            [thirds[2], lanes(stat_left_new.astype(BF16))],
-            [stat_right_new.astype(BF16), lanes(left_blocks.reshape(-1, block_left))],
+        right_2, stat_left_columns, stat_right_rows = run(
+            2, [thirds[2], lanes(stat_left_new.astype(BF16))], [stat_right_new.astype(BF16)]
         )
         left = side_by_side(left.reshape(n_tensor, n_shard * rows_left, block_left))
         right_columns = stacked(jnp.concatenate([right_0, right_1, right_2], axis=1))
@@ -314,7 +363,9 @@
         moment_turned = dot(basis_strip, stacked(moment_right), 0, 0)
         second_new = 0.95 * second_moment + 0.05 * grad_turned * grad_turned
         scaled = (moment_turned / (jnp.sqrt(second_new) + 1e-08)).astype(BF16)
-        back_half = scatter_sum(dot(scaled, right_columns, 1, 1), t, n_tensor).astype(BF16)
+        terms = dot(scaled, right_columns, 1, 1).reshape(rows_left, n_tensor // 2, 2, block_hidden)
+        terms = pick(terms, core, 2) + swap(pick(terms, 1 - core, 2), 1, n_tensor)
+        back = pick(terms, t // 2, 1)
 
         def left_basis(stat_left_all):
             stat_all = side_by_side(stat_left_all.reshape(n_tensor, n_shard * rows_left, block_left))
@@ -339,7 +390,11 @@
         for step in range(NS_ITERS - 1):
             iterate_half = iterate.astype(BF16)
             upper, lower = jnp.split(iterate_half, 2)
-            (upper,) = run(5 + 2 * step, [upper], [])
+            if step == 0:
+                upper, back_there = run(5, [upper], [], [pick(terms, 1 - t // 2, 1)])
+                back_half = (back + back_there).astype(BF16)
+            else:
+                (upper,) = run(5 + 2 * step, [upper], [])
             upper = stacked(upper)
             mine_upper = gram_half(iterate_half, upper, core, n_tensor)
             if step == 0:
@@ -351,6 +406,8 @@
                 lower, there_upper = run(6 + 2 * step, [lower], [], [mine_upper.astype(BF16)])
             lower = stacked(lower)
             mine_lower = gram_half(iterate_half, lower, core, n_tensor)
+            if step == NS_ITERS - 2:
+                mine_lower, stat_left_all = lax.optimization_barrier((mine_lower, stat_left_all))
             there_lower = swap(mine_lower.astype(BF16), n_tensor // 2, n_tensor)
             halves = gram_whole(mine_upper, there_upper)
             change = apply_gram(halves, upper, core)

time: 407 us -> 387 us (0.951)
  waiting for transfers between devices: 24.5 us -> 9.5 us
    ppermute x13 -> x12, waiting for transfers between devices: 24.5 us -> 9.5 us  [swap(): lax.ppermute(array, 'tensor', [(i, i ^ bit) for i in range(n_tensor)])]
  transfers between devices with their start and end apart: 13 -> 12, of which waited for: 6 -> 6; matrix products, arithmetic and copies ran while one was open for 14% -> 13% of each run, Pallas kernels for 7% -> 9%
where the time goes in v2:
time: 387 us; the launch traced here: 386 us
  Pallas kernels  263 us (68%)
  matrix products  66.8 us (17%)
  local copies, waits for them, and re-layouts  25.6 us (7%)
  other arithmetic  12.2 us (3%)
  waiting for transfers between devices  9.5 us (2%)
  starting transfers between devices  5.46 us (1%)
  between operations  3.98 us (1%)
    pallas_call x7, Pallas kernels, gather(): pl.pallas_call(functools.partial(gather_kernel, n_shard // 2, n_tensor, l...  263 us
    dot_general x22, matrix products, dot(): lax.dot_general(a, b, (((ca,), (cb,)), ((), ())), preferred_element_type=...  66.8 us
    ppermute x12, waiting for transfers between devices, swap(): lax.ppermute(array, 'tensor', [(i, i ^ bit) for i in range(n_tensor)])  9.5 us
  transfers between devices with their start and end apart: 12, of which 6 were waited for; matrix products, arithmetic and copies ran while one was open for 13% of the time, Pallas kernels for 9%

profile of v2, /device:TPU:0, one launch (start us, length us, event | category | flops | bytes accessed | tf_op | source)
XLA Modules:
  0.0 386.4 jit_solution(15113999487488601352)
XLA Ops:
  0.7 0.9 convert_element_type.90
  1.6 0.7 reshape.82.refs_1_
  2.3 1.4 convert.5
  3.7 0.8 fusion.79
  4.5 0.8 fusion.77
  5.3 40.9 %gather.7 = (bf16[8,96,768]{2,1,0:T(8,128)(2,1)}, bf16[8,144,128]{2,1,0:T(8,128)(2,1)}, bf16[8,128,768]{2,1,0:T(8,128)(2,1)}, bf16[4,96,768]{2,1,0:T(8,128)(2,1)}, bf16[4,96,768]{2,1,0:T(8,128)(2,1)}) custom-call(bf16[96,768]{1,0:T(8,128)(2,1)} %refs_3_.1, bf16[144,128]{1,0:T(8,128)(2,1)} %reshape.82.refs_1_, bf16[128,768]{1,0:T(8,128)(2,1)} %get-tuple-element.72.refs_2_, ...), custom_call_target="tpu_custom_call" | custom-call | tf_op jit(solution)/shard_map/gather/pallas_call | solution.py:229
  46.2 1.8 convolution_bitcast_fusion
  49.3 0.9 constant_dynamic-slice_fusion.refs_2_
  50.1 36.2 %gather.8 = (bf16[8,128,768]{2,1,0:T(8,128)(2,1)}, bf16[4,1152,128]{2,1,0:T(8,128)(2,1)}, bf16[768,384]{1,0:T(8,128)(2,1)}) custom-call(bf16[128,768]{1,0:T(8,128)(2,1)} %get-tuple-element.71.refs_0_, bf16[1152,128]{1,0:T(8,128)(2,1)} %bitcast.107, bf16[768,384]{1,0:T(8,128)(2,1)} %constant_dynamic-slice_fusion.refs_2_), custom_call_target="tpu_custom_call" | custom-call | tf_op jit(solution)/shard_map/gather/pallas_call | solution.py:229
  86.3 3.1 fusion.81
  89.4 1.3 constant_dynamic-update-slice_fusion.2
  91.4 1.3 constant_dynamic-update-slice_fusion.1
  92.7 2.7 collective-permute-done.1
  95.4 0.7 fusion.76
  96.1 0.7 reshape.85.refs_1_
  96.8 27.7 %gather.9 = (bf16[8,128,768]{2,1,0:T(8,128)(2,1)}, bf16[8,144,128]{2,1,0:T(8,128)(2,1)}, bf16[4,384,768]{2,1,0:T(8,128)(2,1)}) custom-call(bf16[128,768]{1,0:T(8,128)(2,1)} %get-tuple-element.73.refs_0_, bf16[144,128]{1,0:T(8,128)(2,1)} %reshape.85.refs_1_, bf16[384,768]{1,0:T(8,128)(2,1)} %get-tuple-element.78.refs_2_), custom_call_target="tpu_custom_call" | custom-call | tf_op jit(solution)/shard_map/gather/pallas_call | solution.py:229
  124.5 3.0 copy.18
  127.5 2.7 constant_dynamic-update-slice_fusion
  130.2 6.2 %multiply_reduce_fusion.1 = (f32[]{:T(128)}, bf16[384,768]{1,0:T(8,128)(2,1)}, f32[384,768]{1,0:T(8,128)}) fusion(bf16[384,3072]{0,1:T(8,128)(2,1)S(1)} %bitcast.75, bf16[3072,768]{1,0:T(8,128)(2,1)} %bitcast.8), kind=kOutput, calls=%fused_computation.30 | convolution fusion | flops 1812824064 | bytes 8847364 | tf_op jit(solution)/shard_map/dot_general | solution.py:16
  136.4 1.2 broadcast_in_dim.3.refs_1_
  137.7 52.9 %gather.10 = (bf16[8,384,768]{2,1,0:T(8,128)(2,1)}, f32[8,8,128]{2,1,0:T(8,128)}) custom-call(bf16[384,768]{1,0:T(8,128)(2,1)} %get-tuple-element.68.refs_0_, f32[8,128]{1,0:T(8,128)} %broadcast_in_dim.3.refs_1_), custom_call_target="tpu_custom_call" | custom-call | tf_op jit(solution)/shard_map/gather/pallas_call | solution.py:229
  190.6 4.1 %convolution_convert_fusion = bf16[384,1536]{1,0:T(8,128)(2,1)} fusion(bf16[384,768]{1,0:T(8,128)(2,1)} %get-tuple-element.68.refs_0_, bf16[3072,768]{1,0:T(8,128)(2,1)} %bitcast.81, s32[]{:T(128)S(6)} %select_n.94), kind=kOutput, calls=%fused_computation | convolution fusion | flops 906559488 | bytes 4128772 | tf_op jit(solution)/shard_map/dot_general | solution.py:16
  194.8 1.0 copy-done.15
  195.8 0.9 copy.25
  196.7 0.9 reshape.91
  197.6 1.5 copy.21
  199.1 1.4 slice_reduce_fusion
  200.5 3.5 convolution_convert_fusion.4
  204.0 0.7 fusion.80
  206.1 2.7 collective-permute-start.3
  208.8 0.8 collective-permute-done.3
  210.3 4.2 %fusion.82 = (bf16[384,1536]{1,0:T(8,128)(2,1)}, f32[384,1536]{1,0:T(8,128)S(1)}) fusion(bf16[384,1536]{1,0:T(8,128)(2,1)} %collective-permute-done.4, bf16[384,768]{1,0:T(8,128)(2,1)S(1)} %copy-done.1, bf16[3072,768]{1,0:T(8,128)(2,1)} %bitcast.82, s32[]{:T(128)S(6)} %select_n.93), kind=kOutput, calls=%fused_computation.106 | convolution fusion | flops 907739136 | bytes 7667716 | tf_op jit(solution)/shard_map/dot_general | solution.py:16
  214.5 30.3 %gather.11 = (bf16[8,96,768]{2,1,0:T(8,128)(2,1)}, bf16[8,96,768]{2,1,0:T(8,128)(2,1)}, bf16[384,1536]{1,0:T(8,128)(2,1)}) custom-call(bf16[96,768]{1,0:T(8,128)(2,1)} %get-tuple-element.77.refs_0_, bf16[96,768]{1,0:T(8,128)(2,1)} %get-tuple-element.76.refs_1_, bf16[384,1536]{1,0:T(8,128)(2,1)} %get-tuple-element.81.refs_2_), custom_call_target="tpu_custom_call" | custom-call | tf_op jit(solution)/shard_map/gather/pallas_call | solution.py:229
  244.8 1.8 multiply_convert_fusion
  246.7 2.0 fusion.39
  248.8 4.1 %fusion.37 = f32[96,2,2,768]{3,0,2,1:T(8,128)S(1)} fusion(bf16[2,2,768,768]{3,2,1,0:T(8,128)(2,1)} %bitcast.18, bf16[768,768]{1,0:T(8,128)(2,1)S(1)} %bitcast.101, f32[96,768]{1,0:T(8,128)} %fusion.39, bf16[768,768]{0,1:T(8,128)(2,1)} %bitcast.86, s32[]{:T(128)S(6)} %select_n.95), kind=kOutput, calls=%fused_computation.52 | convolution fusion | flops 566452224 | bytes 7520260 | tf_op jit(solution)/shard_map/dot_general | solution.py:16
  253.4 1.8 collective-permute-done.6
  255.1 1.1 bitcast_add_fusion
  256.2 0.7 dynamic-slice_bitcast_fusion.1.refs_1_
  257.0 3.2 fusion
  260.2 3.8 fusion.83
  264.0 0.9 fusion.78
  264.9 33.2 %gather.12 = (bf16[8,192,768]{2,1,0:T(8,128)(2,1)}, f32[96,768]{1,0:T(8,128)}) custom-call(bf16[192,768]{1,0:T(8,128)(2,1)} %get-tuple-element.69.refs_0_, f32[96,768]{1,0:T(8,128)} %dynamic-slice_bitcast_fusion.1.refs_1_), custom_call_target="tpu_custom_call" | custom-call | tf_op jit(solution)/shard_map/gather/pallas_call | solution.py:229
  298.1 2.0 convolution_convert_fusion.3
  300.2 0.7 fusion.40.refs_1_
  300.9 1.3 collective-permute-done.7
  302.2 2.8 fusion.84
  305.0 41.9 %gather.13 = (bf16[8,192,768]{2,1,0:T(8,128)(2,1)}, bf16[8,96,768]{2,1,0:T(8,128)(2,1)}, bf16[4,1152,128]{2,1,0:T(8,128)(2,1)}, bf16[384,768]{1,0:T(8,128)(2,1)}) custom-call(bf16[192,768]{1,0:T(8,128)(2,1)} %get-tuple-element.70.refs_0_, bf16[96,768]{1,0:T(8,128)(2,1)} %fusion.40.refs_1_, bf16[1152,128]{1,0:T(8,128)(2,1)} %bitcast.106, ...), custom_call_target="tpu_custom_call" | custom-call | tf_op jit(solution)/shard_map/gather/pallas_call | solution.py:229
  346.9 2.9 convolution_convert_fusion.2
  350.4 2.6 fusion.43
  353.0 1.7 convert_add_fusion.1
  354.7 2.7 reshape.98
  357.4 1.7 copy.22
  359.2 4.9 %multiply_reduce_fusion = (f32[]{:T(128)}, f32[768,768]{1,0:T(8,128)}) fusion(bf16[768,768]{0,1:T(8,128)(2,1)} %bitcast.100, bf16[768,768]{0,1:T(8,128)(2,1)} %bitcast.88), kind=kOutput, calls=%fused_computation.2 | convolution fusion | flops 907149312 | bytes 4718596 | tf_op jit(solution)/shard_map/dot_general | solution.py:16
  364.7 0.9 convert_element_type.110
  365.6 1.3 collective-permute-start.9
  366.9 7.7 %fusion.85 = (bf16[768,768]{1,0:T(8,128)(2,1)S(1)}, f32[768,768]{1,0:T(8,128)}) fusion(f32[768,768]{1,0:T(8,128)} %get-tuple-element.88, f32[]{:T(128)S(6)} %sqrt.11), kind=kOutput, calls=%fused_computation.109 | convolution fusion | flops 1817837568 | bytes 5898244 | tf_op jit(solution)/shard_map/dot_general | solution.py:16
  374.6 2.2 fusion.17
  376.8 2.2 fusion.26
  379.7 1.6 collective-permute-done.9
  381.3 1.2 add_convert_fusion
  383.2 1.3 collective-permute-done.11
  384.5 0.6 convolution_add_fusion
  385.2 1.2 multiply_subtract_fusion.1
  (71 shorter events, 4.7 us)
Async XLA Ops:
  2.3 2.2 copy-start.4
  2.3 2.2 copy-start.19
  3.7 42.5 %copy-start.5 = (bf16[96,768]{1,0:T(8,128)(2,1)S(1)}, bf16[96,768]{1,0:T(8,128)(2,1)}, u32[]{:S(2)}) copy-start(bf16[96,768]{1,0:T(8,128)(2,1)} %refs_3_.1) | copy-start | bytes 442372
  48.0 1.3 copy-start
  48.8 37.5 %copy-start.12 = (f32[384,768]{1,0:T(8,128)S(1)}, f32[384,768]{1,0:T(8,128)}, u32[]{:S(2)}) copy-start(f32[384,768]{1,0:T(8,128)} %param.11) | copy-start | bytes 3538948
  48.8 41.9 %collective-permute-start = (f32[96,2,192]{2,0,1:T(8,128)S(1)}, f32[96,2,192]{2,0,1:T(8,128)S(1)}, u32[]{:S(2)}, u32[]{:S(2)}) collective-permute-start(f32[96,2,192]{2,0,1:T(8,128)S(1)} %bitcast.108), channel_id=1, source_target_pairs={{0,1},{1,0},{2,3},{3,2},{4,5},{5,4},{6,7},{7,6},{8,9},{9,8},{10,11... | collective-permute-start | bytes 442376 | tf_op jit(solution)/shard_map/ppermute | solution.py:264
  86.3 3.1 copy-start.9
  89.4 2.0 copy-start.10
  90.7 4.7 %collective-permute-start.1 = (f32[96,1,192]{2,0,1:T(8,128)S(1)}, f32[96,1,192]{2,0,1:T(8,128)S(1)}, u32[]{:S(2)}, u32[]{:S(2)}) collective-permute-start(f32[96,1,192]{2,0,1:T(8,128)S(1)} %constant_dynamic-slice_fusion.1), channel_id=1, source_target_pairs={{0,2},{1,3},{2,0},{3,1},{4,6},{5,7},{6,4},{7,5},{8,10},{9,11},{10,... | collective-permute-start | bytes 221192 | tf_op jit(solution)/shard_map/ppermute | solution.py:264
  91.4 4.0 %copy-start.22 = (f32[96,192]{1,0:T(8,128)S(1)}, f32[96,192]{1,0:T(8,128)}, u32[]{:S(2)}) copy-start(f32[96,192]{1,0:T(8,128)} %param.10) | copy-start | bytes 221188
  190.6 4.1 %copy-start.16 = (bf16[4,96,768]{2,1,0:T(8,128)(2,1)S(1)}, bf16[4,96,768]{2,1,0:T(8,128)(2,1)}, u32[]{:S(2)}) copy-start(bf16[4,96,768]{2,1,0:T(8,128)(2,1)} %get-tuple-element.44) | copy-start | bytes 1769476
  194.7 1.1 copy-start.15
  194.7 15.6 %collective-permute-start.4 = (bf16[384,1536]{1,0:T(8,128)(2,1)}, bf16[384,1536]{1,0:T(8,128)(2,1)}, u32[]{:S(2)}, u32[]{:S(2)}) collective-permute-start(bf16[384,1536]{1,0:T(8,128)(2,1)} %convolution_convert_fusion), channel_id=1, source_target_pairs={{0,1},{1,0},{2,3},{3,2},{4,5},{5,4},{6,7},{7,6},{8,9},{9,8},{10,11... | collective-permute-start | bytes 3538952 | tf_op jit(solution)/shard_map/ppermute | solution.py:264
  194.7 2.0 copy-start.13
  197.6 2.9 copy-start.17
  200.4 4.3 %collective-permute-start.2 = (f32[]{:T(128)}, f32[]{:T(128)}, u32[]{:S(2)}, u32[]{:S(2)}) collective-permute-start(f32[]{:T(128)} %slice_reduce_fusion), channel_id=1, source_target_pairs={{0,1},{1,0},{2,3},{3,2},{4,5},{5,4},{6,7},{7,6},{8,9},{9,8},{10,11... | collective-permute-start | bytes 20 | tf_op jit(solution)/shard_map/ppermute | solution.py:264
  200.5 9.8 %copy-start.1 = (bf16[384,768]{1,0:T(8,128)(2,1)S(1)}, bf16[384,768]{1,0:T(8,128)(2,1)}, u32[]{:S(2)}) copy-start(bf16[384,768]{1,0:T(8,128)(2,1)} %get-tuple-element.68.refs_0_) | copy-start | bytes 1769476
  206.1 3.6 collective-permute-start.3
  244.8 1.9 copy-start.11
  244.8 1.9 copy-start.21
  246.6 2.2 copy-start.14
  246.6 10.4 %collective-permute-start.5 = (bf16[384,1536]{1,0:T(8,128)(2,1)S(1)}, bf16[384,1536]{1,0:T(8,128)(2,1)}, u32[]{:S(2)}, u32[]{:S(2)}) collective-permute-start(bf16[384,1536]{1,0:T(8,128)(2,1)S(1)} %multiply_convert_fusion), channel_id=1, source_target_pairs={{0,1},{1,0},{2,3},{3,2},{4,5},{5,4},{6,7},{7,6},{8,9},{9,8},{10,11... | collective-permute-start | bytes 3538952 | tf_op jit(solution)/shard_map/ppermute | solution.py:264
  252.9 2.2 collective-permute-start.6
  257.0 3.2 copy-start.2
  298.1 2.1 copy-start.20
  300.1 2.1 collective-permute-start.7
  346.9 2.9 copy-start.18
  349.7 3.3 collective-permute-start.8
  349.7 3.3 copy-start.7
  349.9 26.9 %collective-permute-start.10 = (bf16[384,768]{1,0:T(8,128)(2,1)S(1)}, bf16[384,768]{1,0:T(8,128)(2,1)}, u32[]{:S(2)}, u32[]{:S(2)}) collective-permute-start(bf16[384,768]{1,0:T(8,128)(2,1)S(1)} %add_convert_fusion.1), channel_id=1, source_target_pairs={{0,1},{1,0},{2,3},{3,2},{4,5},{5,4},{6,7},{7,6},{8,9},{9,8},{10,11... | collective-permute-start | bytes 1769480 | tf_op jit(solution)/shard_map/ppermute | solution.py:264
  365.6 15.7 %collective-permute-start.9 = (bf16[384,768]{1,0:T(8,128)(2,1)}, bf16[384,768]{1,0:T(8,128)(2,1)}, u32[]{:S(2)}, u32[]{:S(2)}) collective-permute-start(bf16[384,768]{1,0:T(8,128)(2,1)} %convert_element_type.110), channel_id=1, source_target_pairs={{0,2},{1,3},{2,0},{3,1},{4,6},{5,7},{6,4},{7,5},{8,10},{9,11},{10,... | collective-permute-start | bytes 1769480 | tf_op jit(solution)/shard_map/ppermute | solution.py:264
  376.8 2.2 copy-start.6
  379.7 2.9 copy-start.8
  382.4 2.1 collective-permute-start.11
  383.2 2.0 copy-start.3

commit v3 on v2

--- a/solution.py
+++ b/solution.py
@@ -316,21 +316,15 @@
         moment_new = 0.9 * moment + 0.1 * gradient.astype(F32)
         third = rows_right // 3
         thirds = [part(basis_right, k, third, 0).astype(BF16) for k in range(3)]
-        panel, left_blocks, right_0, grad_rows, moment_rows = run(
-            0,
-            [gradient, lanes(basis_left.astype(BF16)), thirds[0]],
-            [gradient, moment_new.astype(BF16)],
+        panel, left_blocks, right_0 = run(
+            0, [gradient, lanes(basis_left.astype(BF16)), thirds[0]], []
         )
         panel = stacked(panel)
         first = s * rows_right
         owner = first // block_hidden
         strip = lax.dynamic_slice_in_dim(panel, first - owner * block_hidden, rows_right, 1)
-        right_1, left, strip = run(
-            1,
-            [thirds[1]],
-            [lanes(left_blocks.reshape(-1, block_left))],
-            casts=[strip],
-            cast_ratio=(rows_right, block_hidden),
+        right_1, strip = run(
+            1, [thirds[1]], [], casts=[strip], cast_ratio=(rows_right, block_hidden)
         )
         stat_right_new = 0.95 * stat_right + 0.05 * dot(strip, panel, 0, 0)
         cross_left = scatter_sum(dot(gradient, panel, 1, 1), t, n_tensor)
@@ -338,16 +332,20 @@
         right_2, stat_left_columns, stat_right_rows = run(
             2, [thirds[2], lanes(stat_left_new.astype(BF16))], [stat_right_new.astype(BF16)]
         )
-        left = side_by_side(left.reshape(n_tensor, n_shard * rows_left, block_left))
         right_columns = stacked(jnp.concatenate([right_0, right_1, right_2], axis=1))
 
         power = dot(side_by_side(stat_right_rows), right_columns, 1, 0)
         power_half = power.astype(BF16)
         square = jnp.full((8, 128), jnp.sum(power * power), F32)
+        power_panel, squares, left, grad_rows, moment_rows = run(
+            3,
+            [power_half, square],
+            [lanes(left_blocks.reshape(-1, block_left)), gradient, moment_new.astype(BF16)],
+        )
+        left = side_by_side(left.reshape(n_tensor, n_shard * rows_left, block_left))
         rotated = jnp.concatenate([side_by_side(grad_rows), side_by_side(moment_rows)])
         rotated = dot(rotated, right_columns, 1, 0).astype(BF16)
         grad_right, moment_right = rotated[:rows_left], rotated[rows_left:]
-        power_panel, squares = run(3, [power_half, square], [])
         power_panel = stacked(power_panel)
 
         square = whole_sum(jnp.sum(squares[:, 0, 0]), n_tensor)

time: 387 us -> 378 us (0.977)
  Pallas kernels: 263 us -> 254 us
    pallas_call x7, Pallas kernels: 263 us -> 254 us  [gather(): pl.pallas_call(functools.partial(gather_kernel, n_shard // 2, n_tensor, l...]
  transfers between devices with their start and end apart: 12 -> 12, of which waited for: 6 -> 6; matrix products, arithmetic and copies ran while one was open for 13% -> 14% of each run, Pallas kernels for 9% -> 7%
where the time goes in v3:
time: 378 us; the launch traced here: 377 us
  Pallas kernels  254 us (67%)
  matrix products  66.4 us (18%)
  local copies, waits for them, and re-layouts  25 us (7%)
  other arithmetic  12.2 us (3%)
  waiting for transfers between devices  9.94 us (3%)
  starting transfers between devices  5.74 us (2%)
  between operations  3.82 us (1%)
    pallas_call x7, Pallas kernels, gather(): pl.pallas_call(functools.partial(gather_kernel, n_shard // 2, n_tensor, l...  254 us
    dot_general x22, matrix products, dot(): lax.dot_general(a, b, (((ca,), (cb,)), ((), ())), preferred_element_type=...  66.4 us
    ppermute x12, waiting for transfers between devices, swap(): lax.ppermute(array, 'tensor', [(i, i ^ bit) for i in range(n_tensor)])  9.94 us
  transfers between devices with their start and end apart: 12, of which 6 were waited for; matrix products, arithmetic and copies ran while one was open for 14% of the time, Pallas kernels for 7%

profile of v3, /device:TPU:0, one launch (start us, length us, event | category | flops | bytes accessed | tf_op | source)
XLA Modules:
  0.0 376.8 jit_solution(13116014669005688783)
XLA Ops:
  0.7 0.9 convert_element_type.90
  1.6 0.7 reshape.82.refs_1_
  2.3 1.3 convert.5
  3.6 0.8 fusion.79
  4.5 40.7 %gather.7 = (bf16[8,96,768]{2,1,0:T(8,128)(2,1)}, bf16[8,144,128]{2,1,0:T(8,128)(2,1)}, bf16[8,128,768]{2,1,0:T(8,128)(2,1)}) custom-call(bf16[96,768]{1,0:T(8,128)(2,1)} %refs_3_.1, bf16[144,128]{1,0:T(8,128)(2,1)} %reshape.82.refs_1_, bf16[128,768]{1,0:T(8,128)(2,1)} %get-tuple-element.72.refs_2_), custom_call_target="tpu_custom_call" | custom-call | tf_op jit(solution)/shard_map/gather/pallas_call | solution.py:229
  45.2 1.8 convolution_bitcast_fusion
  47.9 0.8 fusion.76
  48.8 0.9 constant_dynamic-slice_fusion.refs_1_
  49.6 27.0 %gather.8 = (bf16[8,128,768]{2,1,0:T(8,128)(2,1)}, bf16[768,384]{1,0:T(8,128)(2,1)}) custom-call(bf16[128,768]{1,0:T(8,128)(2,1)} %get-tuple-element.71.refs_0_, bf16[768,384]{1,0:T(8,128)(2,1)} %constant_dynamic-slice_fusion.refs_1_), custom_call_target="tpu_custom_call" | custom-call | tf_op jit(solution)/shard_map/gather/pallas_call | solution.py:229
  76.7 3.1 fusion.81
  79.8 1.3 constant_dynamic-update-slice_fusion.2
  81.7 1.3 constant_dynamic-update-slice_fusion.1
  83.0 2.8 collective-permute-done.1
  85.8 0.7 fusion.77
  86.5 0.7 reshape.85.refs_1_
  87.2 27.8 %gather.9 = (bf16[8,128,768]{2,1,0:T(8,128)(2,1)}, bf16[8,144,128]{2,1,0:T(8,128)(2,1)}, bf16[4,384,768]{2,1,0:T(8,128)(2,1)}) custom-call(bf16[128,768]{1,0:T(8,128)(2,1)} %get-tuple-element.73.refs_0_, bf16[144,128]{1,0:T(8,128)(2,1)} %reshape.85.refs_1_, bf16[384,768]{1,0:T(8,128)(2,1)} %get-tuple-element.78.refs_2_), custom_call_target="tpu_custom_call" | custom-call | tf_op jit(solution)/shard_map/gather/pallas_call | solution.py:229
  115.0 3.0 copy.18
  118.0 2.7 constant_dynamic-update-slice_fusion
  120.7 6.2 %multiply_reduce_fusion.1 = (f32[]{:T(128)}, bf16[384,768]{1,0:T(8,128)(2,1)}, f32[384,768]{1,0:T(8,128)}) fusion(bf16[384,3072]{0,1:T(8,128)(2,1)S(1)} %bitcast.75, bf16[3072,768]{1,0:T(8,128)(2,1)} %bitcast.7), kind=kOutput, calls=%fused_computation.30 | convolution fusion | flops 1812824064 | bytes 8847364 | tf_op jit(solution)/shard_map/dot_general | solution.py:16
  126.9 1.3 broadcast_in_dim.3.refs_1_
  128.2 53.1 %gather.10 = (bf16[8,384,768]{2,1,0:T(8,128)(2,1)}, f32[8,8,128]{2,1,0:T(8,128)}, bf16[4,1152,128]{2,1,0:T(8,128)(2,1)}, bf16[4,96,768]{2,1,0:T(8,128)(2,1)}, bf16[4,96,768]{2,1,0:T(8,128)(2,1)}) custom-call(bf16[384,768]{1,0:T(8,128)(2,1)} %get-tuple-element.68.refs_0_, f32[8,128]{1,0:T(8,128)} %broadcast_in_dim.3.refs_1_, bf16[1152,128]{1,0:T(8,128)(2,1)} %bitcast.107, ...), custom_call_target="tpu_custom_call" | custom-call | tf_op jit(solution)/shard_map/gather/pallas_call | solution.py:229
  181.4 3.9 %convolution_convert_fusion = bf16[384,1536]{1,0:T(8,128)(2,1)} fusion(bf16[384,768]{1,0:T(8,128)(2,1)S(1)} %copy-done.1, bf16[3072,768]{1,0:T(8,128)(2,1)} %bitcast.81, s32[]{:T(128)S(6)} %select_n.94), kind=kOutput, calls=%fused_computation | convolution fusion | flops 906559488 | bytes 4128772 | tf_op jit(solution)/shard_map/dot_general | solution.py:16
  185.3 1.4 slice_reduce_fusion
  187.3 2.7 reshape.91
  190.0 1.5 copy.21
  191.5 3.4 convolution_convert_fusion.4
  194.9 0.7 fusion.80
  196.9 3.2 collective-permute-start.3
  201.2 4.2 %fusion.82 = (bf16[384,1536]{1,0:T(8,128)(2,1)}, f32[384,1536]{1,0:T(8,128)S(1)}) fusion(bf16[384,1536]{1,0:T(8,128)(2,1)} %collective-permute-done.4, bf16[384,768]{1,0:T(8,128)(2,1)S(1)} %copy-done.1, bf16[3072,768]{1,0:T(8,128)(2,1)} %bitcast.82, s32[]{:T(128)S(6)} %select_n.93), kind=kOutput, calls=%fused_computation.106 | convolution fusion | flops 907739136 | bytes 7667716 | tf_op jit(solution)/shard_map/dot_general | solution.py:16
  205.4 29.3 %gather.11 = (bf16[8,96,768]{2,1,0:T(8,128)(2,1)}, bf16[8,96,768]{2,1,0:T(8,128)(2,1)}, bf16[384,1536]{1,0:T(8,128)(2,1)}) custom-call(bf16[96,768]{1,0:T(8,128)(2,1)} %get-tuple-element.77.refs_0_, bf16[96,768]{1,0:T(8,128)(2,1)} %get-tuple-element.76.refs_1_, bf16[384,1536]{1,0:T(8,128)(2,1)} %get-tuple-element.81.refs_2_), custom_call_target="tpu_custom_call" | custom-call | tf_op jit(solution)/shard_map/gather/pallas_call | solution.py:229
  234.7 1.8 multiply_convert_fusion
  236.6 2.0 fusion.39
  238.7 4.1 %fusion.37 = f32[96,2,2,768]{3,0,2,1:T(8,128)S(1)} fusion(bf16[2,2,768,768]{3,2,1,0:T(8,128)(2,1)} %bitcast.18, bf16[768,768]{1,0:T(8,128)(2,1)S(1)} %bitcast.101, f32[96,768]{1,0:T(8,128)} %fusion.39, bf16[768,768]{0,1:T(8,128)(2,1)} %bitcast.86, s32[]{:T(128)S(6)} %select_n.95), kind=kOutput, calls=%fused_computation.52 | convolution fusion | flops 566452224 | bytes 7520260 | tf_op jit(solution)/shard_map/dot_general | solution.py:16
  243.3 1.8 collective-permute-done.6
  245.0 1.1 bitcast_add_fusion
  246.2 0.8 dynamic-slice_bitcast_fusion.1.refs_1_
  246.9 3.2 fusion
  250.1 3.8 %fusion.83 = (bf16[384,768]{1,0:T(8,128)(2,1)S(1)}, f32[384,768]{1,0:T(8,128)}) fusion(f32[384,768]{1,0:T(8,128)S(1)} %fusion, bf16[384,1536]{1,0:T(8,128)(2,1)S(1)} %multiply_convert_fusion, bf16[3072,768]{1,0:T(8,128)(2,1)} %bitcast.84, s32[]{:T(128)S(6)} %select_n.93, f32[384,768]{1,0:T(8,128)S(1)} %copy-done.2, f32[]{:T(128)S(6)} %sqrt.9), kind=kOutput, calls=%fused_computation.107 | convolution fusion | flops 907739136 | bytes 7667720 | tf_op jit(solution)/shard_map/dot_general | solution.py:16
  254.0 0.9 fusion.78
  254.8 33.3 %gather.12 = (bf16[8,192,768]{2,1,0:T(8,128)(2,1)}, f32[96,768]{1,0:T(8,128)}) custom-call(bf16[192,768]{1,0:T(8,128)(2,1)} %get-tuple-element.69.refs_0_, f32[96,768]{1,0:T(8,128)} %dynamic-slice_bitcast_fusion.1.refs_1_), custom_call_target="tpu_custom_call" | custom-call | tf_op jit(solution)/shard_map/gather/pallas_call | solution.py:229
  288.2 2.0 convolution_convert_fusion.3
  290.3 0.7 fusion.40.refs_1_
  291.0 1.3 collective-permute-done.7
  292.2 2.8 fusion.84
  295.0 42.5 %gather.13 = (bf16[8,192,768]{2,1,0:T(8,128)(2,1)}, bf16[8,96,768]{2,1,0:T(8,128)(2,1)}, bf16[4,1152,128]{2,1,0:T(8,128)(2,1)}, bf16[384,768]{1,0:T(8,128)(2,1)}) custom-call(bf16[192,768]{1,0:T(8,128)(2,1)} %get-tuple-element.70.refs_0_, bf16[96,768]{1,0:T(8,128)(2,1)} %fusion.40.refs_1_, bf16[1152,128]{1,0:T(8,128)(2,1)} %bitcast.106, ...), custom_call_target="tpu_custom_call" | custom-call | tf_op jit(solution)/shard_map/gather/pallas_call | solution.py:229
  337.6 2.9 convolution_convert_fusion.2
  340.5 0.6 collective-permute-start.10
  341.1 2.6 fusion.43
  343.7 1.7 convert_add_fusion.1
  345.4 2.7 reshape.98
  348.1 1.5 copy.22
  349.6 4.9 %multiply_reduce_fusion = (f32[]{:T(128)}, f32[768,768]{1,0:T(8,128)}) fusion(bf16[768,768]{0,1:T(8,128)(2,1)} %bitcast.100, bf16[768,768]{0,1:T(8,128)(2,1)} %bitcast.88), kind=kOutput, calls=%fused_computation.2 | convolution fusion | flops 907149312 | bytes 4718596 | tf_op jit(solution)/shard_map/dot_general | solution.py:16
  355.2 0.9 convert_element_type.110
  356.0 0.7 collective-permute-start.9
  356.8 7.6 %fusion.85 = (bf16[768,768]{1,0:T(8,128)(2,1)S(1)}, f32[768,768]{1,0:T(8,128)}) fusion(f32[768,768]{1,0:T(8,128)} %get-tuple-element.88, f32[]{:T(128)S(6)} %sqrt.11), kind=kOutput, calls=%fused_computation.109 | convolution fusion | flops 1817837568 | bytes 5898244 | tf_op jit(solution)/shard_map/dot_general | solution.py:16
  364.4 2.2 fusion.17
  366.6 2.2 fusion.26
  368.8 0.6 convolution_add_fusion.1
  369.4 2.3 collective-permute-done.9
  371.7 1.2 add_convert_fusion
  373.0 0.6 fusion.20
  373.6 1.3 collective-permute-done.11
  375.0 0.6 convolution_add_fusion
  375.6 1.2 multiply_subtract_fusion.1
  (65 shorter events, 3.5 us)
Async XLA Ops:
  3.6 41.6 %copy-start.4 = (bf16[96,768]{1,0:T(8,128)(2,1)S(1)}, bf16[96,768]{1,0:T(8,128)(2,1)}, u32[]{:S(2)}) copy-start(bf16[96,768]{1,0:T(8,128)(2,1)} %refs_3_.1) | copy-start | bytes 442372
  47.0 1.0 copy-start.16
  47.4 1.4 copy-start
  47.8 33.3 %collective-permute-start = (f32[96,2,192]{2,0,1:T(8,128)S(1)}, f32[96,2,192]{2,0,1:T(8,128)S(1)}, u32[]{:S(2)}, u32[]{:S(2)}) collective-permute-start(f32[96,2,192]{2,0,1:T(8,128)S(1)} %bitcast.108), channel_id=1, source_target_pairs={{0,1},{1,0},{2,3},{3,2},{4,5},{5,4},{6,7},{7,6},{8,9},{9,8},{10,11... | collective-permute-start | bytes 442376 | tf_op jit(solution)/shard_map/ppermute | solution.py:264
  48.8 27.9 %copy-start.11 = (f32[384,768]{1,0:T(8,128)S(1)}, f32[384,768]{1,0:T(8,128)}, u32[]{:S(2)}) copy-start(f32[384,768]{1,0:T(8,128)} %param.11) | copy-start | bytes 3538948
  76.7 3.1 copy-start.8
  79.8 2.0 copy-start.9
  81.1 4.7 %collective-permute-start.1 = (f32[96,1,192]{2,0,1:T(8,128)S(1)}, f32[96,1,192]{2,0,1:T(8,128)S(1)}, u32[]{:S(2)}, u32[]{:S(2)}) collective-permute-start(f32[96,1,192]{2,0,1:T(8,128)S(1)} %constant_dynamic-slice_fusion.1), channel_id=1, source_target_pairs={{0,2},{1,3},{2,0},{3,1},{4,6},{5,7},{6,4},{7,5},{8,10},{9,11},{10,... | collective-permute-start | bytes 221192 | tf_op jit(solution)/shard_map/ppermute | solution.py:264
  81.7 4.1 %copy-start.19 = (f32[96,192]{1,0:T(8,128)S(1)}, f32[96,192]{1,0:T(8,128)}, u32[]{:S(2)}) copy-start(f32[96,192]{1,0:T(8,128)} %param.10) | copy-start | bytes 221188
  126.9 54.4 %copy-start.1 = (bf16[384,768]{1,0:T(8,128)(2,1)S(1)}, bf16[384,768]{1,0:T(8,128)(2,1)}, u32[]{:S(2)}) copy-start(bf16[384,768]{1,0:T(8,128)(2,1)} %get-tuple-element.68.refs_0_) | copy-start | bytes 1769476
  181.4 5.8 %copy-start.14 = (bf16[4,96,768]{2,1,0:T(8,128)(2,1)S(1)}, bf16[4,96,768]{2,1,0:T(8,128)(2,1)}, u32[]{:S(2)}) copy-start(bf16[4,96,768]{2,1,0:T(8,128)(2,1)} %get-tuple-element.44) | copy-start | bytes 1769476
  185.3 1.9 copy-start.13
  185.3 15.9 %collective-permute-start.4 = (bf16[384,1536]{1,0:T(8,128)(2,1)}, bf16[384,1536]{1,0:T(8,128)(2,1)}, u32[]{:S(2)}, u32[]{:S(2)}) collective-permute-start(bf16[384,1536]{1,0:T(8,128)(2,1)} %convolution_convert_fusion), channel_id=1, source_target_pairs={{0,1},{1,0},{2,3},{3,2},{4,5},{5,4},{6,7},{7,6},{8,9},{9,8},{10,11... | collective-permute-start | bytes 3538952 | tf_op jit(solution)/shard_map/ppermute | solution.py:264
  186.7 8.9 %collective-permute-start.2 = (f32[]{:T(128)}, f32[]{:T(128)}, u32[]{:S(2)}, u32[]{:S(2)}) collective-permute-start(f32[]{:T(128)} %slice_reduce_fusion), channel_id=1, source_target_pairs={{0,1},{1,0},{2,3},{3,2},{4,5},{5,4},{6,7},{7,6},{8,9},{9,8},{10,11... | collective-permute-start | bytes 20 | tf_op jit(solution)/shard_map/ppermute | solution.py:264
  196.9 3.7 collective-permute-start.3
  234.7 1.9 copy-start.10
  234.7 1.9 copy-start.18
  236.5 2.2 copy-start.12
  236.5 10.4 %collective-permute-start.5 = (bf16[384,1536]{1,0:T(8,128)(2,1)S(1)}, bf16[384,1536]{1,0:T(8,128)(2,1)}, u32[]{:S(2)}, u32[]{:S(2)}) collective-permute-start(bf16[384,1536]{1,0:T(8,128)(2,1)S(1)} %multiply_convert_fusion), channel_id=1, source_target_pairs={{0,1},{1,0},{2,3},{3,2},{4,5},{5,4},{6,7},{7,6},{8,9},{9,8},{10,11... | collective-permute-start | bytes 3538952 | tf_op jit(solution)/shard_map/ppermute | solution.py:264
  242.8 2.2 collective-permute-start.6
  246.9 3.2 copy-start.2
  288.2 2.1 copy-start.17
  290.1 2.1 collective-permute-start.7
  337.5 2.9 copy-start.15
  340.4 3.3 collective-permute-start.8
  340.4 3.3 copy-start.6
  340.5 26.0 %collective-permute-start.10 = (bf16[384,768]{1,0:T(8,128)(2,1)S(1)}, bf16[384,768]{1,0:T(8,128)(2,1)}, u32[]{:S(2)}, u32[]{:S(2)}) collective-permute-start(bf16[384,768]{1,0:T(8,128)(2,1)S(1)} %add_convert_fusion.1), channel_id=1, source_target_pairs={{0,1},{1,0},{2,3},{3,2},{4,5},{5,4},{6,7},{7,6},{8,9},{9,8},{10,11... | collective-permute-start | bytes 1769480 | tf_op jit(solution)/shard_map/ppermute | solution.py:264
  356.0 15.7 %collective-permute-start.9 = (bf16[384,768]{1,0:T(8,128)(2,1)}, bf16[384,768]{1,0:T(8,128)(2,1)}, u32[]{:S(2)}, u32[]{:S(2)}) collective-permute-start(bf16[384,768]{1,0:T(8,128)(2,1)} %convert_element_type.110), channel_id=1, source_target_pairs={{0,2},{1,3},{2,0},{3,1},{4,6},{5,7},{6,4},{7,5},{8,10},{9,11},{10,... | collective-permute-start | bytes 1769480 | tf_op jit(solution)/shard_map/ppermute | solution.py:264
  366.6 2.2 copy-start.5
  369.4 3.5 copy-start.7
  372.9 2.1 collective-permute-start.11
  373.6 2.0 copy-start.3
